TPU v7x, 128 devices: a whole 4x4x4 slice. The times are simulated.
128 devices in a mesh: ctx: 8 (over x, z_hi), grp: 16 (over y, z_lo, core).
Axes of the slice: x: 4, y: 4, z: 4 (z_hi: 2, z_lo: 2; z = z_hi * 2 + z_lo), core: 2. Of those that a mesh axis runs over, the one named last changes fastest.
Arguments:
- tail_q: bfloat16 [16, 512, 8192], P('grp', 'ctx'), may hold values from -6 to 6
- prompt_kv: bfloat16 [16, 4480, 2048], P('grp', 'ctx'), may hold values from -6 to 6
- dest_owner: int32 [16, 8, 35, 1], P('grp', 'ctx'), may hold values from 0 to 15; in each aligned block of 35 rows (0 to 34, 35 to 69, ..., all dimensions but the last counted through in order) at most 5 rows name the same one
- dest_row: int32 [16, 8, 35], P('grp', 'ctx'), may hold values from 0 to 3
- dec_q: bfloat16 [64, 2, 8192], P('grp'), may hold values from -6 to 6
- new_kv: bfloat16 [64, 2, 2048], P('grp'), may hold values from -6 to 6
- res_kv: bfloat16 [64, 1024, 2048], P('grp', 'ctx'), may hold values from -6 to 6
- lens: int32 [64], P('grp'), may hold values from 1 to 1024, 32768 in all
Outputs:
- prefill_out: bfloat16 [16, 512, 8192], P('grp', 'ctx')
- decode_out: bfloat16 [64, 2, 8192], P('grp', None, 'ctx')
Inputs may be any that keep to these rules, and one draw needn't show every extreme that they name: `dest_owner`: among the 35 blocks of one prompt shard (one device), no owner is named more than 5 times; in some shards one owner is named exactly 5 times.
All inputs are finite; a program needn't handle non-finite values. No bound on the sum of `lens` on one device may be relied on, other than what follows from the above.
Results may differ from a plain program's by a relative error of at most 0.012.
Values may be sent and summed in bfloat16 or wider, within the bound.
No kernel may reach another device: no remote copies, remote signals or barrier semaphores. Data moves between devices by JAX's collectives and lax.ppermute only.
A program may use at most 128 MiB of HBM per device.

v0:
```python
import math

import jax
import jax.numpy as jnp
from jax import lax
from jax.sharding import PartitionSpec as P

H = 64
KVH = 8
HD = 128
PRE_DEV = 496
TAIL_DEV = 64
BLK = 16
ROW_GRP = 4
RES_DEV = 128
GROUP = 8
KVD = 1024
QD = 8192
SEQ_DEV = 560
NB = 35


MASKED = -jnp.inf
FLOOR = -1e30


def merged(value, axis, join):
    pieces = jax.tree.map(lambda part: lax.all_gather(part, axis), value)
    head = jax.tree.map(lambda part: part[0], pieces)
    tail = jax.tree.map(lambda part: part[1:], pieces)
    subtotal, _ = lax.scan(lambda subtotal, share: (join(subtotal, share), None), head, tail)
    return subtotal


def key_allowed(key_index, query_pos):
    offset = key_index % SEQ_DEV
    tail_pos = jnp.where(offset >= PRE_DEV, key_index // SEQ_DEV * TAIL_DEV + offset - PRE_DEV, -1)
    return tail_pos[None, :] <= query_pos[:, None]


def join_parts(first_part, second_part):
    peak_first, total_first, mixed_first = first_part
    peak_second, total_second, mixed_second = second_part
    peak = jnp.maximum(peak_first, peak_second)
    fade_first = jnp.exp(peak_first - peak)
    fade_second = jnp.exp(peak_second - peak)
    total = total_first * fade_first + total_second * fade_second
    mixed = mixed_first * fade_first[..., None] + mixed_second * fade_second[..., None]
    return (peak, total, mixed)


def local(tail_q, prompt_kv, dest_owner, dest_row, dec_q, new_kv, res_kv, lens):
    scale = 1.0 / math.sqrt(HD)
    ctx_pos = lax.axis_index("ctx")
    n_ctx = lax.axis_size("ctx")
    n_grp = lax.axis_size("grp")
    per_owner = max(2, (2 * NB + n_grp - 1) // n_grp)
    own_pos = ctx_pos * TAIL_DEV + jnp.arange(TAIL_DEV)
    local_kv = prompt_kv[0]
    q_heads = tail_q[0].reshape(TAIL_DEV, KVH, GROUP, HD)
    start_peak = jnp.full((KVH, TAIL_DEV, GROUP), FLOOR, jnp.float32)
    piece = lax.all_gather(prompt_kv, "ctx", axis=1, tiled=True)
    peak = start_peak
    piece = piece[0]
    allowed = key_allowed(jnp.arange(piece.shape[0]), own_pos)

    def one_head(head):
        query = lax.dynamic_index_in_dim(q_heads, head, 1, keepdims=False)
        keys = lax.dynamic_slice_in_dim(piece, head * HD, HD, 1)
        values = lax.dynamic_slice_in_dim(piece, KVD + head * HD, HD, 1)
        scores = jnp.einsum("cgd,pd->cgp", query, keys, preferred_element_type=jnp.float32) * scale
        scores = jnp.where(allowed[:, None, :], scores, MASKED)
        old_peak = peak[head]
        new_peak = jnp.maximum(old_peak, jnp.max(scores, axis=-1))
        weights = jnp.exp(scores - new_peak[..., None])
        new_total = jnp.sum(weights, axis=-1)
        new_mixed = jnp.einsum("cgp,pd->cgd", weights, values, preferred_element_type=jnp.float32)
        return (new_peak, new_total, new_mixed)

    peak, total, mixed = lax.map(one_head, jnp.arange(KVH))
    prefill_out = (
        (mixed / total[..., None])
        .transpose(1, 0, 2, 3)
        .reshape(TAIL_DEV, QD)
        .astype(jnp.bfloat16)[None]
    )
    owners = dest_owner.reshape(NB)
    targets = dest_row.reshape(NB)
    slots = n_grp * per_owner
    same_owner = owners[:, None] == owners[None, :]
    earlier = jnp.arange(NB)[None, :] < jnp.arange(NB)[:, None]
    rank = jnp.sum(same_owner & earlier, axis=1)
    slot = owners * per_owner + rank
    match = slot[None, :] == jnp.arange(slots)[:, None]
    filled = jnp.any(match, axis=1)
    source = jnp.sum(jnp.where(match, jnp.arange(NB)[None, :], 0), axis=1)
    row_of = jnp.where(filled, jnp.sum(jnp.where(match, targets[None, :], 0), axis=1), -1)
    blocks = local_kv.reshape(NB, BLK, 2 * KVD)
    outgoing = jnp.where(filled[:, None, None], jnp.take(blocks, source, axis=0), 0)
    outgoing = outgoing.reshape(n_grp, per_owner * BLK, 2 * KVD)
    labels = row_of.astype(jnp.bfloat16).reshape(n_grp, per_owner)
    arrived, arrived_rows = (
        lax.all_to_all(outgoing, "grp", split_axis=0, concat_axis=0, tiled=True),
        lax.all_to_all(labels, "grp", split_axis=0, concat_axis=0, tiled=True),
    )
    q_rows = dec_q.reshape(ROW_GRP, 2, KVH, GROUP, HD)
    res_keys = res_kv[:, :, :KVD].reshape(ROW_GRP, RES_DEV, KVH, HD)
    res_values = res_kv[:, :, KVD:].reshape(ROW_GRP, RES_DEV, KVH, HD)
    live = ctx_pos * RES_DEV + jnp.arange(RES_DEV)[None, :] < lens[:, None]
    score_res = (
        jnp.einsum("rtkgd,rpkd->rtkgp", q_rows, res_keys, preferred_element_type=jnp.float32)
        * scale
    )
    score_res = jnp.where(live[:, None, None, None, :], score_res, MASKED)
    moved = arrived.reshape(slots, BLK, 2 * KVD)
    moved_rows = arrived_rows.reshape(slots).astype(jnp.int32)
    valid = moved_rows >= 0
    chosen = jnp.maximum(moved_rows, 0)
    q_slots = jnp.take(q_rows, chosen, axis=0)
    moved_keys = moved[:, :, :KVD].reshape(slots, BLK, KVH, HD)
    moved_values = moved[:, :, KVD:].reshape(slots, BLK, KVH, HD)
    score_moved = (
        jnp.einsum("stkgd,sbkd->stkgb", q_slots, moved_keys, preferred_element_type=jnp.float32)
        * scale
    )
    score_moved = jnp.where(valid[:, None, None, None, None], score_moved, MASKED)
    owner_match = moved_rows[None, :] == jnp.arange(ROW_GRP)[:, None]
    slot_peak = jnp.max(score_moved, axis=-1)
    moved_peak = jnp.max(
        jnp.where(owner_match[:, :, None, None, None], slot_peak[None], MASKED), axis=1
    )
    local_peak = jnp.maximum(jnp.maximum(jnp.max(score_res, axis=-1), moved_peak), FLOOR)
    weight_res = jnp.exp(score_res - local_peak[..., None])
    weight_moved = jnp.exp(score_moved - jnp.take(local_peak, chosen, axis=0)[..., None])
    one_hot = owner_match.astype(jnp.float32)
    part_total = jnp.sum(weight_res, axis=-1) + jnp.einsum(
        "rs,stkg->rtkg", one_hot, jnp.sum(weight_moved, axis=-1)
    )
    slot_mixed = jnp.einsum(
        "stkgb,sbkd->stkgd", weight_moved, moved_values, preferred_element_type=jnp.float32
    )
    part_mixed = jnp.einsum(
        "rtkgp,rpkd->rtkgd", weight_res, res_values, preferred_element_type=jnp.float32
    )
    part_mixed = part_mixed + jnp.einsum("rs,stkgd->rtkgd", one_hot, slot_mixed)
    part_peak = local_peak.reshape(ROW_GRP, 2, H)
    part_total = part_total.reshape(ROW_GRP, 2, H)
    part_mixed = part_mixed.reshape(ROW_GRP, 2, H, HD)
    heads_dev = H // n_ctx
    first_head = ctx_pos * heads_dev
    peak_all, total_all, mixed_all = merged((part_peak, part_total, part_mixed), "ctx", join_parts)
    top = lax.dynamic_slice_in_dim(peak_all, first_head, heads_dev, 2)
    row_total = lax.dynamic_slice_in_dim(total_all, first_head, heads_dev, 2)
    row_mixed = lax.dynamic_slice_in_dim(mixed_all, first_head, heads_dev, 2)
    own_heads = first_head + jnp.arange(heads_dev)
    key_head = own_heads // GROUP
    q_own = lax.dynamic_slice_in_dim(dec_q.reshape(ROW_GRP, 2, H, HD), first_head, heads_dev, 2)
    new_keys = jnp.take(new_kv[:, :, :KVD].reshape(ROW_GRP, 2, KVH, HD), key_head, axis=2)
    new_values = jnp.take(new_kv[:, :, KVD:].reshape(ROW_GRP, 2, KVH, HD), key_head, axis=2)
    score_new = (
        jnp.einsum("rthd,ruhd->rthu", q_own, new_keys, preferred_element_type=jnp.float32) * scale
    )
    causal = jnp.arange(2)[None, :] <= jnp.arange(2)[:, None]
    score_new = jnp.where(causal[None, :, None, :], score_new, MASKED)
    final_peak = jnp.maximum(top, jnp.max(score_new, axis=-1))
    fade_old = jnp.exp(top - final_peak)
    weight_new = jnp.exp(score_new - final_peak[..., None])
    final_total = row_total * fade_old + jnp.sum(weight_new, axis=-1)
    final_mixed = row_mixed * fade_old[..., None] + jnp.einsum(
        "rthu,ruhd->rthd", weight_new, new_values, preferred_element_type=jnp.float32
    )
    decode_out = (
        (final_mixed / final_total[..., None])
        .astype(jnp.bfloat16)
        .reshape(ROW_GRP, 2, heads_dev * HD)
    )
    return (prefill_out, decode_out)


def solution(mesh):
    return jax.shard_map(
        local,
        mesh=mesh,
        in_specs=(
            P("grp", "ctx", None),
            P("grp", "ctx", None),
            P("grp", "ctx", None, None),
            P("grp", "ctx", None),
            P("grp", None, None),
            P("grp", None, None),
            P("grp", "ctx", None),
            P("grp"),
        ),
        out_specs=(P("grp", "ctx", None), P("grp", None, "ctx")),
        check_vma=False,
    )
```

profile of v0, /device:TPU:1, one launch (start us, length us, event | category | flops | bytes accessed | tf_op | source)
XLA Modules:
  0.0 536.1 jit_solution(9862161308717518359)
XLA Ops:
  10.3 7.3 %all-to-all-start = ((bf16[16,1,5]{2,1,0:T(2,128)(2,1)}), bf16[16,1,5]{2,1,0:T(2,128)(2,1)S(1)}, u32[]{:S(2)}, u32[]{:S(2)}) async-start(bf16[16,1,5]{2,1,0:T(2,128)(2,1)} %convert_element_type.76), calls=%async_computation | async-start | bytes 16384 | tf_op jit(solution)/shard_map/all_to_all | solution.py:104
  18.2 7.3 %gather_fusion = bf16[80,16,2048]{2,1,0:T(8,128)(2,1)} fusion(bf16[35,16,2048]{2,1,0:T(8,128)(2,1)} %bitcast.169, s32[1024]{0:T(1024)S(1)} %pad_clamp_fusion.2), kind=kCustom, calls=%fused_computation.2 | custom fusion | bytes 10486080 | tf_op jit(solution)/shard_map/jit(_take)/gather | solution.py:99
  25.6 5.5 %fusion.20 = bf16[16,80,2048]{2,1,0:T(8,128)(2,1)} fusion(pred[16,80]{1,0:T(8,128)(4,1)S(1)} %broadcast_in_dim.227, pred[16,80]{1,0:T(8,128)(4,1)S(1)} %broadcast_in_dim.223, bf16[16,80,2048]{2,1,0:T(8,128)(2,1)} %bitcast.170), kind=kLoop, calls=%fused_computation.39 | loop fusion | flops 5242880 | bytes 10488320 | tf_op jit(solution)/shard_map/jit(_where)/select_n | solution.py:99
  31.1 5.8 %all-to-all-start.1 = ((bf16[16,80,2048]{2,1,0:T(8,128)(2,1)}), bf16[16,80,2048]{2,1,0:T(8,128)(2,1)}, u32[]{:S(2)}, u32[]{:S(2)}) async-start(bf16[16,80,2048]{2,1,0:T(8,128)(2,1)} %fusion.20), calls=%async_computation.1 | async-start | bytes 10485760 | tf_op jit(solution)/shard_map/all_to_all | solution.py:103
  42.6 2.6 gather_fusion.1
  45.1 64.0 %all-to-all-done.1 = bf16[16,80,2048]{2,1,0:T(8,128)(2,1)} async-done(((bf16[16,80,2048]{2,1,0:T(8,128)(2,1)}), bf16[16,80,2048]{2,1,0:T(8,128)(2,1)}, u32[]{:S(2)}, u32[]{:S(2)}) %all-to-all-start.1) | async-done | bytes 5242912 | tf_op jit(solution)/shard_map/all_to_all | solution.py:103
  109.2 3.1 fusion.83
  114.7 3.9 bitcast_reduce_fusion
  122.7 2.5 fusion.34
  132.3 28.2 %all_gather.13 = f32[8,4,2,64]{3,1,2,0:T(4,128)S(1)} all-gather(f32[1,4,2,64]{3,1,2,0:T(4,128)S(1)} %copy.232), channel_id=1, replica_groups=mesh['ctx'=8,'grp'=16] {'ctx'}, dimensions={0}, use_global_device_ids=true | all-gather | bytes 18432 | tf_op jit(solution)/shard_map/all_gather | solution.py:28
  160.8 5.6 %fusion.25 = bf16[80,2,8,8]{3,1,2,0:T(2,128)(2,1)S(1)} fusion(f32[80,8,16,2,8]{2,4,3,1,0:T(8,128)} %get-tuple-element.311, f32[80,2,8,8]{3,1,2,0:T(2,128)S(1)} %copy-done.2, pred[80]{0:T(512)(128)(4,1)S(1)} %copy-done.11), kind=kLoop, calls=%fused_computation.44 | loop fusion | flops 645120 | bytes 716880 | tf_op jit(solution)/shard_map/reduce_sum | solution.py:137
  166.7 28.0 %all_gather.14 = f32[8,4,2,64]{3,1,2,0:T(4,128)S(1)} all-gather(f32[1,4,2,64]{3,1,2,0:T(4,128)S(1)} %copy.238), channel_id=1, replica_groups=mesh['ctx'=8,'grp'=16] {'ctx'}, dimensions={0}, use_global_device_ids=true | all-gather | bytes 18432 | tf_op jit(solution)/shard_map/all_gather | solution.py:28
  197.4 2.3 while.29
  201.8 190.6 %all-gather.3.cloned.1.call-done = bf16[1,4480,2048]{2,1,0:T(8,128)(2,1)} async-done(((bf16[1,560,2048]{2,1,0:T(8,128)(2,1)}), bf16[1,4480,2048]{2,1,0:T(8,128)(2,1)}) %all-gather.3.cloned.1.call-update) | async-done | bytes 18350096 | tf_op jit(solution)/shard_map/all_gather | solution.py:62
  392.4 133.4 %while.30 = (s32[]{:T(128)}, f32[8,64,8]{2,1,0:T(8,128)S(1)}, f32[8,64,8,128]{3,2,1,0:T(8,128)}, s32[8]{0:T(128)S(1)}, bf16[64,8,8,128]{3,2,1,0:T(8,128)(2,1)S(1...) while((s32[]{:T(128)}, f32[8,64,8]{2,1,0:T(8,128)S(1)}, ...), condition=%wide.region_3.4_spmd.clone, body=%wide.region_0.3_spmd.clone.sunk | while | flops 1188453888 | bytes 67582032 | solution.py:80
  395.8 3.6 fusion.99
  403.0 6.0 %fusion.101 = f32[8,64,8,128]{3,2,1,0:T(8,128)} fusion(f32[8,64,8,128]{3,2,1,0:T(8,128)} %get-tuple-element.441, s32[]{:T(128)S(6)} %copy.333, f32[64,8,4480]{2,1,0:T(8,128)} %copy-done, f32[64,8]{1,0:T(8,128)S(1)} %broadcast_maximum_fusion.2, bf16[4480,2048]{1,0:T(8,128)(2,1)} %get-tuple-element.459, s32[]{:T(128)S(6)} %select_n.253), kind=kOutput, calls=%fused_computation.23.clone.1 | convolution fusion | flops 589496320 | bytes 10586120 | tf_op jit(solution)/shard_map/while/body/eval_jaxpr/cgp,pd->cgd/dot_general | solution.py:77
  412.4 3.6 fusion.99
  419.6 6.1 %fusion.101 = f32[8,64,8,128]{3,2,1,0:T(8,128)} fusion(f32[8,64,8,128]{3,2,1,0:T(8,128)} %get-tuple-element.441, s32[]{:T(128)S(6)} %copy.333, f32[64,8,4480]{2,1,0:T(8,128)} %copy-done, f32[64,8]{1,0:T(8,128)S(1)} %broadcast_maximum_fusion.2, bf16[4480,2048]{1,0:T(8,128)(2,1)} %get-tuple-element.459, s32[]{:T(128)S(6)} %select_n.253), kind=kOutput, calls=%fused_computation.23.clone.1 | convolution fusion | flops 589496320 | bytes 10586120 | tf_op jit(solution)/shard_map/while/body/eval_jaxpr/cgp,pd->cgd/dot_general | solution.py:77
  429.1 3.6 fusion.99
  434.1 2.2 copy-done
  436.3 6.2 %fusion.101 = f32[8,64,8,128]{3,2,1,0:T(8,128)} fusion(f32[8,64,8,128]{3,2,1,0:T(8,128)} %get-tuple-element.441, s32[]{:T(128)S(6)} %copy.333, f32[64,8,4480]{2,1,0:T(8,128)} %copy-done, f32[64,8]{1,0:T(8,128)S(1)} %broadcast_maximum_fusion.2, bf16[4480,2048]{1,0:T(8,128)(2,1)} %get-tuple-element.459, s32[]{:T(128)S(6)} %select_n.253), kind=kOutput, calls=%fused_computation.23.clone.1 | convolution fusion | flops 589496320 | bytes 10586120 | tf_op jit(solution)/shard_map/while/body/eval_jaxpr/cgp,pd->cgd/dot_general | solution.py:77
  445.9 3.6 fusion.99
  453.1 6.1 %fusion.101 = f32[8,64,8,128]{3,2,1,0:T(8,128)} fusion(f32[8,64,8,128]{3,2,1,0:T(8,128)} %get-tuple-element.441, s32[]{:T(128)S(6)} %copy.333, f32[64,8,4480]{2,1,0:T(8,128)} %copy-done, f32[64,8]{1,0:T(8,128)S(1)} %broadcast_maximum_fusion.2, bf16[4480,2048]{1,0:T(8,128)(2,1)} %get-tuple-element.459, s32[]{:T(128)S(6)} %select_n.253), kind=kOutput, calls=%fused_computation.23.clone.1 | convolution fusion | flops 589496320 | bytes 10586120 | tf_op jit(solution)/shard_map/while/body/eval_jaxpr/cgp,pd->cgd/dot_general | solution.py:77
  462.6 3.6 fusion.99
  469.8 6.0 %fusion.101 = f32[8,64,8,128]{3,2,1,0:T(8,128)} fusion(f32[8,64,8,128]{3,2,1,0:T(8,128)} %get-tuple-element.441, s32[]{:T(128)S(6)} %copy.333, f32[64,8,4480]{2,1,0:T(8,128)} %copy-done, f32[64,8]{1,0:T(8,128)S(1)} %broadcast_maximum_fusion.2, bf16[4480,2048]{1,0:T(8,128)(2,1)} %get-tuple-element.459, s32[]{:T(128)S(6)} %select_n.253), kind=kOutput, calls=%fused_computation.23.clone.1 | convolution fusion | flops 589496320 | bytes 10586120 | tf_op jit(solution)/shard_map/while/body/eval_jaxpr/cgp,pd->cgd/dot_general | solution.py:77
  479.2 3.6 fusion.99
  486.4 6.1 %fusion.101 = f32[8,64,8,128]{3,2,1,0:T(8,128)} fusion(f32[8,64,8,128]{3,2,1,0:T(8,128)} %get-tuple-element.441, s32[]{:T(128)S(6)} %copy.333, f32[64,8,4480]{2,1,0:T(8,128)} %copy-done, f32[64,8]{1,0:T(8,128)S(1)} %broadcast_maximum_fusion.2, bf16[4480,2048]{1,0:T(8,128)(2,1)} %get-tuple-element.459, s32[]{:T(128)S(6)} %select_n.253), kind=kOutput, calls=%fused_computation.23.clone.1 | convolution fusion | flops 589496320 | bytes 10586120 | tf_op jit(solution)/shard_map/while/body/eval_jaxpr/cgp,pd->cgd/dot_general | solution.py:77
  495.9 3.6 fusion.99
  503.1 6.1 %fusion.101 = f32[8,64,8,128]{3,2,1,0:T(8,128)} fusion(f32[8,64,8,128]{3,2,1,0:T(8,128)} %get-tuple-element.441, s32[]{:T(128)S(6)} %copy.333, f32[64,8,4480]{2,1,0:T(8,128)} %copy-done, f32[64,8]{1,0:T(8,128)S(1)} %broadcast_maximum_fusion.2, bf16[4480,2048]{1,0:T(8,128)(2,1)} %get-tuple-element.459, s32[]{:T(128)S(6)} %select_n.253), kind=kOutput, calls=%fused_computation.23.clone.1 | convolution fusion | flops 589496320 | bytes 10586120 | tf_op jit(solution)/shard_map/while/body/eval_jaxpr/cgp,pd->cgd/dot_general | solution.py:77
  512.5 3.6 fusion.99
  519.7 6.0 %fusion.101 = f32[8,64,8,128]{3,2,1,0:T(8,128)} fusion(f32[8,64,8,128]{3,2,1,0:T(8,128)} %get-tuple-element.441, s32[]{:T(128)S(6)} %copy.333, f32[64,8,4480]{2,1,0:T(8,128)} %copy-done, f32[64,8]{1,0:T(8,128)S(1)} %broadcast_maximum_fusion.2, bf16[4480,2048]{1,0:T(8,128)(2,1)} %get-tuple-element.459, s32[]{:T(128)S(6)} %select_n.253), kind=kOutput, calls=%fused_computation.23.clone.1 | convolution fusion | flops 589496320 | bytes 10586120 | tf_op jit(solution)/shard_map/while/body/eval_jaxpr/cgp,pd->cgd/dot_general | solution.py:77
  (198 shorter events, 66.3 us)
Async XLA Ops:
  10.3 20.8 %all-to-all-start = ((bf16[16,1,5]{2,1,0:T(2,128)(2,1)}), bf16[16,1,5]{2,1,0:T(2,128)(2,1)S(1)}, u32[]{:S(2)}, u32[]{:S(2)}) async-start(bf16[16,1,5]{2,1,0:T(2,128)(2,1)} %convert_element_type.76), calls=%async_computation | async-start | bytes 16384 | tf_op jit(solution)/shard_map/all_to_all | solution.py:104
  31.1 6.1 %copy-start.8 = (bf16[4,2,8192]{2,1,0:T(2,128)(2,1)S(1)}, bf16[4,2,8192]{2,1,0:T(2,128)(2,1)}, u32[]{:S(2)}) copy-start(bf16[4,2,8192]{2,1,0:T(2,128)(2,1)} %param.18) | copy-start | bytes 393220
  31.1 78.1 %all-to-all-start.1 = ((bf16[16,80,2048]{2,1,0:T(8,128)(2,1)}), bf16[16,80,2048]{2,1,0:T(8,128)(2,1)}, u32[]{:S(2)}, u32[]{:S(2)}) async-start(bf16[16,80,2048]{2,1,0:T(8,128)(2,1)} %fusion.20), calls=%async_computation.1 | async-start | bytes 10485760 | tf_op jit(solution)/shard_map/all_to_all | solution.py:103
  36.9 157.8 %all-gather.5.cloned.1.call-start = ((), (), s32[]{:S(2)}) async-start(), calls=%async_computation.3 | async-start | bytes 2359296 | tf_op jit(solution)/shard_map/all_gather | solution.py:28
  39.1 2.0 copy-start.12
  45.1 76.1 %copy-start.10 = (pred[80]{0:T(512)(128)(4,1)}, pred[80]{0:T(512)(128)(4,1)S(1)}, u32[]{:S(2)}) copy-start(pred[80]{0:T(512)(128)(4,1)S(1)} %get-tuple-element.308) | copy-start | bytes 244
  112.9 1.7 copy-start.3
  119.9 2.4 slice-start
  120.3 1.1 copy-start.1
  120.3 2.4 slice-start.1
  125.2 1.5 copy-start.5
  125.2 1.5 copy-start.6
  126.7 2.3 copy-start.4
  127.4 1.8 copy-start.9
  128.1 32.6 %copy-start.2 = (f32[80,2,8,8]{3,1,2,0:T(2,128)S(1)}, f32[80,2,8,8]{3,1,2,0:T(2,128)}, u32[]{:S(2)}) copy-start(f32[80,2,8,8]{3,1,2,0:T(2,128)} %copy-done.1) | copy-start | bytes 122884
  128.2 32.6 %copy-start.11 = (pred[80]{0:T(512)(128)(4,1)S(1)}, pred[80]{0:T(512)(128)(4,1)}, u32[]{:S(2)}) copy-start(pred[80]{0:T(512)(128)(4,1)} %copy-done.10) | copy-start | bytes 244
  128.2 264.2 %all-gather.3.cloned.1.call-start = ((), (), s32[]{:S(2)}) async-start(), calls=%async_computation.2 | async-start | bytes 20643840 | tf_op jit(solution)/shard_map/all_gather | solution.py:62
  160.5 6.0 %copy-start.7 = (f32[8,4,2,64]{3,1,2,0:T(4,128)}, f32[8,4,2,64]{3,1,2,0:T(4,128)S(1)}, u32[]{:S(2)}) copy-start(f32[8,4,2,64]{3,1,2,0:T(4,128)S(1)} %all_gather.13) | copy-start | bytes 49156
  166.6 30.7 %slice-start.2 = ((f32[8,4,2,64]{3,1,2,0:T(4,128)}), f32[7,4,2,64]{3,1,2,0:T(4,128)S(1)}, s32[]{:S(2)}) async-start(f32[8,4,2,64]{3,1,2,0:T(4,128)} %copy-done.7), calls=%async_computation.6 | async-start | bytes 57344 | tf_op jit(solution)/shard_map/slice | solution.py:30
  399.4 3.6 copy-start
  416.0 3.6 copy-start
  432.7 3.6 copy-start
  449.5 3.6 copy-start
  466.2 3.6 copy-start
  482.8 3.6 copy-start
  499.5 3.6 copy-start
  516.2 3.6 copy-start
Sparse Core Ops, SparseCore 0:
  128.3 61.8 all-gather.4
  192.5 199.8 all-gather.2
where the time goes:
time: 537 us; the launch traced here: 536 us
  waiting for transfers between devices  255 us (47%)
  matrix products  89.7 us (17%)
  blocking collectives  56.1 us (10%)
  local copies, waits for them, and re-layouts  53.6 us (10%)
  other arithmetic  32.1 us (6%)
  loops' own time  21.2 us (4%)
  between operations  14.6 us (3%)
  starting transfers between devices  13.4 us (2%)
    all_gather x1, waiting for transfers between devices, local(): piece = lax.all_gather(prompt_kv, 'ctx', axis=1, tiled=True)  191 us
    all_to_all x1, waiting for transfers between devices, local(): lax.all_to_all(outgoing, 'grp', split_axis=0, concat_axis=0, tiled=True)  64 us
    all_gather x2, blocking collectives, merged(): pieces = jax.tree.map(lambda part: lax.all_gather(part, axis), value)  56.1 us
    dot_general x8, matrix products, one_head(): jnp.einsum('cgp,pd->cgd', weights, values, preferred_element_type=jnp.flo...  48.6 us
    dot_general x8, matrix products, one_head(): jnp.einsum('cgd,pd->cgp', query, keys, preferred_element_type=jnp.float32)  28.8 us
    another operation x1, loops' own time, local(): peak, total, mixed = lax.map(one_head, jnp.arange(KVH))  21 us
    while x16, local copies, waits for them, and re-layouts  17.3 us
    reduce_sum x8, other arithmetic, one_head(): new_total = jnp.sum(weights, axis=-1)  11.2 us
  transfers between devices with their start and end apart: 4, of which 2 were waited for; matrix products, arithmetic and copies ran while one was open for 7% of the time, Pallas kernels for 0%

commit v1 on v0

v1 whole, which is shorter than its diff:
```python
import functools
import math

import jax
import jax.numpy as jnp
from jax import lax
from jax.experimental import pallas as pl
from jax.experimental.pallas import tpu as pltpu
from jax.sharding import PartitionSpec as P

HD = 128
KVH = 8
GROUP = 8
PRE_DEV = 496
TAIL_DEV = 64
BLK = 16
ROW_GRP = 4
RES_DEV = 128
KVD = 1024
SEQ_DEV = 560
N_CTX = 8
N_GRP = 16

KEYS = N_CTX * SEQ_DEV
TAIL = N_CTX * TAIL_DEV
SEND_ROWS = SEQ_DEV + 16
FLAT = N_CTX * SEND_ROWS
Q_ROWS = GROUP * TAIL_DEV
VECS = 2 * GROUP
OWN_VECS = ROW_GRP * VECS
PART_ROWS = OWN_VECS + 16
QPART_ROWS = Q_ROWS + PART_ROWS

FLOOR = -1e30
LOG2E = 1.4426950408889634
COEF = LOG2E / math.sqrt(HD)
VMEM = 56 * 2**20
NT = (((1,), (1,)), ((), ()))


def widen_query(q):
    scaled = q.astype(jnp.float32) * COEF
    high = scaled.astype(jnp.bfloat16)
    low = (scaled - high.astype(jnp.float32)).astype(jnp.bfloat16)
    return jnp.concatenate([high, low], axis=1)


def part_of(acc, peak):
    rows = acc.shape[0]
    total = jnp.maximum(acc[:, HD:], 1.0)
    out = (acc[:, :HD] / total).astype(jnp.bfloat16)
    weight = peak + jnp.log2(total)
    diag = lax.broadcasted_iota(jnp.int32, (rows, HD), 0) == lax.broadcasted_iota(
        jnp.int32, (rows, HD), 1
    )
    line = jnp.sum(jnp.where(diag, weight, 0.0), axis=0, keepdims=True)
    first = line.astype(jnp.bfloat16)
    rest = line - first.astype(jnp.float32)
    second = rest.astype(jnp.bfloat16)
    third = rest - second.astype(jnp.float32)
    place = lax.broadcasted_iota(jnp.int32, (16, HD), 0)
    stats = jnp.where(
        place == 0,
        first.astype(jnp.float32),
        jnp.where(place == 1, second.astype(jnp.float32), jnp.where(place == 2, third, 0.0)),
    )
    return out, stats.astype(jnp.bfloat16)


def pack_kv_kernel(k_ref, v_ref, label_ref, out_ref):
    out_ref[0, :SEQ_DEV, :HD] = k_ref[...]
    out_ref[0, :SEQ_DEV, HD:] = v_ref[...]
    out_ref[0, SEQ_DEV:, :] = label_ref[...]


def pack_kv(kv, labels):
    return pl.pallas_call(
        pack_kv_kernel,
        grid=(KVH,),
        in_specs=[
            pl.BlockSpec((SEQ_DEV, HD), lambda e: (0, e)),
            pl.BlockSpec((SEQ_DEV, HD), lambda e: (0, KVH + e)),
            pl.BlockSpec((16, 2 * HD), lambda e: (0, 0)),
        ],
        out_specs=pl.BlockSpec((1, SEND_ROWS, 2 * HD), lambda e: (e, 0, 0)),
        out_shape=jax.ShapeDtypeStruct((KVH, SEND_ROWS, 2 * HD), jnp.bfloat16),
        cost_estimate=pl.CostEstimate(flops=0, bytes_accessed=4600000, transcendentals=0),
        name="pack_kv",
    )(kv, kv, labels)


def query_res_kernel(live_ref, q_ref, dq_ref, k_ref, v_ref, out_ref, vs_ref):
    for head in range(GROUP):
        out_ref[0, head * TAIL_DEV : (head + 1) * TAIL_DEV, :] = q_ref[
            :, head * HD : (head + 1) * HD
        ]
    keys = k_ref[...].reshape(ROW_GRP * RES_DEV, HD)
    vs_ref[:, :HD] = v_ref[...].reshape(ROW_GRP * RES_DEV, HD)
    vs_ref[:, HD:] = jnp.ones((ROW_GRP * RES_DEV, HD), jnp.bfloat16)
    query = widen_query(dq_ref[0])
    scores = lax.dot_general(query[:, :HD], keys, NT, preferred_element_type=jnp.float32)
    scores += lax.dot_general(query[:, HD:], keys, NT, preferred_element_type=jnp.float32)
    shape = (OWN_VECS, ROW_GRP * RES_DEV)
    row = lax.broadcasted_iota(jnp.int32, shape, 0)
    col = lax.broadcasted_iota(jnp.int32, shape, 1)
    for r in range(ROW_GRP):
        inside = (row >= r * VECS) & (row < (r + 1) * VECS)
        low, high = r * RES_DEV, jnp.clip(live_ref[r], 0, RES_DEV) + r * RES_DEV
        scores = jnp.where(inside & ((col < low) | (col >= high)), -jnp.inf, scores)
    peak = jnp.maximum(jnp.max(scores, axis=1, keepdims=True), FLOOR)
    weights = jnp.exp2(scores - peak).astype(jnp.bfloat16)
    acc = jnp.dot(weights, vs_ref[...], preferred_element_type=jnp.float32)
    out, stats = part_of(acc, peak)
    out_ref[0, Q_ROWS : Q_ROWS + OWN_VECS, :] = out
    out_ref[0, Q_ROWS + OWN_VECS :, :] = stats


def query_res(live, tail_q, dec_vecs, res_kv):
    return pl.pallas_call(
        query_res_kernel,
        grid=(KVH,),
        in_specs=[
            pl.BlockSpec(memory_space=pltpu.SMEM),
            pl.BlockSpec((TAIL_DEV, GROUP * HD), lambda e: (0, e)),
            pl.BlockSpec((1, OWN_VECS, HD), lambda e: (e, 0, 0)),
            pl.BlockSpec((ROW_GRP, RES_DEV, HD), lambda e: (0, 0, e)),
            pl.BlockSpec((ROW_GRP, RES_DEV, HD), lambda e: (0, 0, KVH + e)),
        ],
        out_specs=pl.BlockSpec((1, QPART_ROWS, HD), lambda e: (e, 0, 0)),
        out_shape=jax.ShapeDtypeStruct((KVH, QPART_ROWS, HD), jnp.bfloat16),
        scratch_shapes=[pltpu.VMEM((ROW_GRP * RES_DEV, 2 * HD), jnp.bfloat16)],
        cost_estimate=pl.CostEstimate(flops=500000000, bytes_accessed=4600000, transcendentals=0),
        name="query_res",
    )(live, tail_q, dec_vecs, res_kv, res_kv)


def prefill_kernel(chunks, q_ref, kv_ref, o_ref, k_s, v_s):
    shard = pl.program_id(0)

    @pl.when(shard == 0)
    def _():
        for s in range(N_CTX):
            for dst, src, n in (
                (s * TAIL_DEV, PRE_DEV, TAIL_DEV),
                (TAIL + s * PRE_DEV, 0, PRE_DEV),
            ):
                keys = kv_ref[s, src : src + n, :HD]
                k_s[dst : dst + n, :HD] = keys
                k_s[dst : dst + n, HD:] = keys
                v_s[dst : dst + n, :HD] = kv_ref[s, src : src + n, HD:]
        v_s[:, HD:] = jnp.ones((KEYS, HD), jnp.bfloat16)

    query = widen_query(q_ref[0])
    peak = acc = None
    start = 0
    for n in chunks:
        scores = lax.dot_general(
            query, k_s[start : start + n, :], NT, preferred_element_type=jnp.float32
        )
        if start < TAIL:
            token = (
                lax.broadcasted_iota(jnp.int32, (Q_ROWS, n), 0) % TAIL_DEV + shard * TAIL_DEV
            )
            col = lax.broadcasted_iota(jnp.int32, (Q_ROWS, n), 1) + start
            scores = jnp.where((col > token) & (col < TAIL), -jnp.inf, scores)
        top = jnp.max(scores, axis=1, keepdims=True)
        new_peak = top if peak is None else jnp.maximum(peak, top)
        weights = jnp.exp2(scores - new_peak).astype(jnp.bfloat16)
        mixed = jnp.dot(weights, v_s[start : start + n, :], preferred_element_type=jnp.float32)
        acc = mixed if peak is None else acc * jnp.exp2(peak - new_peak) + mixed
        peak = new_peak
        start += n
    out = (acc[:, :HD] / acc[:, HD:]).astype(jnp.bfloat16)
    for head in range(GROUP):
        o_ref[0, :, head * HD : (head + 1) * HD] = out[head * TAIL_DEV : (head + 1) * TAIL_DEV]


def prefill(queries, kv):
    return pl.pallas_call(
        functools.partial(prefill_kernel, (1024, 1024, 1024, 1408)),
        grid=(N_CTX,),
        in_specs=[
            pl.BlockSpec((1, Q_ROWS, HD), lambda d: (d, 0, 0)),
            pl.BlockSpec((N_CTX, SEND_ROWS, 2 * HD), lambda d: (0, 0, 0)),
        ],
        out_specs=pl.BlockSpec((1, TAIL_DEV, GROUP * HD), lambda d: (d, 0, 0)),
        out_shape=jax.ShapeDtypeStruct((N_CTX, TAIL_DEV, GROUP * HD), jnp.bfloat16),
        scratch_shapes=[
            pltpu.VMEM((KEYS, 2 * HD), jnp.bfloat16),
            pltpu.VMEM((KEYS, 2 * HD), jnp.bfloat16),
        ],
        compiler_params=pltpu.CompilerParams(vmem_limit_bytes=VMEM),
        cost_estimate=pl.CostEstimate(
            flops=30000000000, bytes_accessed=5000000, transcendentals=18000000
        ),
        name="prefill",
    )(queries, kv)


BLK_ROWS = 512
BLK_CHUNK = 1536


def blocks_kernel(q_ref, kv_ref, label_ref, o_ref, k_s, v_s):
    part = pl.program_id(0)

    @pl.when(part == 0)
    def _():
        keys = kv_ref[:, :HD]
        k_s[:, :HD] = keys
        k_s[:, HD:] = keys
        v_s[:, :HD] = kv_ref[:, HD:]
        v_s[:, HD:] = jnp.ones((FLAT, HD), jnp.bfloat16)

    query = widen_query(q_ref[...])
    peak = acc = None
    row = lax.broadcasted_iota(jnp.int32, (BLK_ROWS, BLK_CHUNK), 0) + part * BLK_ROWS
    row = row // VECS
    for start in range(0, FLAT, BLK_CHUNK):
        end = start + BLK_CHUNK
        scores = lax.dot_general(query, k_s[start:end, :], NT, preferred_element_type=jnp.float32)
        scores = jnp.where(label_ref[:, start:end] == row, scores, -jnp.inf)
        top = jnp.maximum(jnp.max(scores, axis=1, keepdims=True), FLOOR)
        new_peak = top if peak is None else jnp.maximum(peak, top)
        weights = jnp.exp2(scores - new_peak).astype(jnp.bfloat16)
        mixed = jnp.dot(weights, v_s[start:end, :], preferred_element_type=jnp.float32)
        acc = mixed if peak is None else acc * jnp.exp2(peak - new_peak) + mixed
        peak = new_peak
    for i in range(BLK_ROWS // OWN_VECS):
        span = slice(i * OWN_VECS, (i + 1) * OWN_VECS)
        out, stats = part_of(acc[span], peak[span])
        o_ref[i, :OWN_VECS, :] = out
        o_ref[i, OWN_VECS:, :] = stats


def blocks(queries, kv, labels):
    rows = queries.shape[0]
    return pl.pallas_call(
        blocks_kernel,
        grid=(rows // BLK_ROWS,),
        in_specs=[
            pl.BlockSpec((BLK_ROWS, HD), lambda i: (i, 0)),
            pl.BlockSpec((FLAT, 2 * HD), lambda i: (0, 0)),
            pl.BlockSpec((1, FLAT), lambda i: (0, 0)),
        ],
        out_specs=pl.BlockSpec((BLK_ROWS // OWN_VECS, PART_ROWS, HD), lambda i: (i, 0, 0)),
        out_shape=jax.ShapeDtypeStruct((rows // OWN_VECS, PART_ROWS, HD), jnp.bfloat16),
        scratch_shapes=[
            pltpu.VMEM((FLAT, 2 * HD), jnp.bfloat16),
            pltpu.VMEM((FLAT, 2 * HD), jnp.bfloat16),
        ],
        compiler_params=pltpu.CompilerParams(vmem_limit_bytes=VMEM),
        cost_estimate=pl.CostEstimate(
            flops=8000000000, bytes_accessed=3000000, transcendentals=4700000
        ),
        name="blocks",
    )(queries, kv, labels)


def finish_kernel(blk_ref, res_ref, q_ref, nk_ref, nv_ref, o_ref):
    shape = (OWN_VECS, HD)
    row = lax.broadcasted_iota(jnp.int32, shape, 0)
    col = lax.broadcasted_iota(jnp.int32, shape, 1)
    diag = row == col
    query = widen_query(q_ref[...])
    keys = jnp.concatenate([nk_ref[...], jnp.zeros((HD - 16, HD), jnp.bfloat16)], axis=0)
    values = jnp.concatenate([nv_ref[...], jnp.zeros((HD - 16, HD), jnp.bfloat16)], axis=0)
    scores = lax.dot_general(query[:, :HD], keys, NT, preferred_element_type=jnp.float32)
    scores += lax.dot_general(query[:, HD:], keys, NT, preferred_element_type=jnp.float32)
    open_ = (col // 2 == row // VECS) & (col % 2 <= row % VECS // GROUP)
    scores = jnp.where(open_, scores, -jnp.inf)
    outs, weights = [], []
    for ref, count, base in ((blk_ref, N_GRP, 0), (res_ref, N_CTX, 0)):
        for i in range(count):
            outs.append(ref[i, base : base + OWN_VECS, :])
            stats = ref[i, base + OWN_VECS : base + PART_ROWS, :].astype(jnp.float32)
            line = jnp.sum(stats[0:8], axis=0, keepdims=True)
            weights.append(jnp.sum(jnp.where(diag, line, 0.0), axis=1, keepdims=True))
    peak = jnp.max(scores, axis=1, keepdims=True)
    for weight in weights:
        peak = jnp.maximum(peak, weight)
    new = jnp.exp2(scores - peak)
    total = jnp.sum(new, axis=1, keepdims=True)
    mixed = jnp.dot(new.astype(jnp.bfloat16), values, preferred_element_type=jnp.float32)
    for out, weight in zip(outs, weights):
        share = jnp.exp2(weight - peak)
        total += share
        mixed += share * out.astype(jnp.float32)
    o_ref[...] = (mixed / total).astype(jnp.bfloat16)


def finish(block_parts, res_parts, queries, new_keys, new_values):
    return pl.pallas_call(
        finish_kernel,
        out_shape=jax.ShapeDtypeStruct((OWN_VECS, HD), jnp.bfloat16),
        cost_estimate=pl.CostEstimate(flops=5000000, bytes_accessed=600000, transcendentals=0),
        name="finish",
    )(block_parts, res_parts, queries, new_keys, new_values)


def place_kernel(in_ref, out_ref):
    out_ref[...] = in_ref[0]


def place(parts):
    return pl.pallas_call(
        place_kernel,
        grid=(KVH,),
        in_specs=[pl.BlockSpec((1, TAIL_DEV, GROUP * HD), lambda e: (e, 0, 0))],
        out_specs=pl.BlockSpec((TAIL_DEV, GROUP * HD), lambda e: (0, e)),
        out_shape=jax.ShapeDtypeStruct((TAIL_DEV, KVH * GROUP * HD), jnp.bfloat16),
        cost_estimate=pl.CostEstimate(flops=0, bytes_accessed=2100000, transcendentals=0),
        name="place",
    )(parts)


def local(tail_q, prompt_kv, dest_owner, dest_row, dec_q, new_kv, res_kv, lens):
    ctx = lax.axis_index("ctx")
    block_row = dest_owner.reshape(-1) * ROW_GRP + dest_row.reshape(-1)
    labels = jnp.pad(jnp.repeat(block_row, BLK), (0, 16), constant_values=-1)
    labels = jnp.pad(labels, (0, 16 * 2 * HD - SEND_ROWS)).reshape(16, 2 * HD)
    sent_kv = pack_kv(prompt_kv[0], labels.astype(jnp.bfloat16))
    got_kv = lax.all_to_all(sent_kv, "ctx", split_axis=0, concat_axis=0, tiled=True)

    dec_vecs = dec_q.reshape(ROW_GRP * 2, KVH, GROUP, HD).transpose(1, 0, 2, 3)
    dec_vecs = dec_vecs.reshape(KVH, OWN_VECS, HD)
    own_vecs = lax.dynamic_index_in_dim(dec_vecs, ctx, 0, keepdims=False)
    spread = jnp.broadcast_to(own_vecs[None], (N_GRP, OWN_VECS, HD))
    all_vecs = lax.all_to_all(spread, "grp", split_axis=0, concat_axis=0, tiled=True)

    sent_q = query_res(lens - ctx * RES_DEV, tail_q[0], dec_vecs, res_kv)
    got_q = lax.all_to_all(sent_q, "ctx", split_axis=0, concat_axis=0, tiled=True)

    got_labels = got_kv[:, SEQ_DEV:, :].reshape(N_CTX, -1)[:, :SEND_ROWS]
    got_labels = got_labels.reshape(1, FLAT).astype(jnp.int32)
    block_parts = blocks(
        all_vecs.reshape(-1, HD), got_kv.reshape(FLAT, 2 * HD), got_labels
    )
    block_parts = lax.all_to_all(block_parts, "grp", split_axis=0, concat_axis=0, tiled=True)

    prefill_parts = prefill(got_q, got_kv)
    prefill_parts = lax.all_to_all(
        prefill_parts, "ctx", split_axis=0, concat_axis=0, tiled=True
    )

    own_new = new_kv.reshape(ROW_GRP * 2, 2, KVH, HD)
    own_new = lax.dynamic_index_in_dim(own_new, ctx, 2, keepdims=False)
    own_new = jnp.pad(own_new, ((0, 8), (0, 0), (0, 0)))
    decode = finish(
        block_parts, got_q[:, Q_ROWS:, :], own_vecs, own_new[:, 0], own_new[:, 1]
    )
    decode_out = decode.reshape(ROW_GRP, 2, GROUP * HD)
    prefill_out = place(prefill_parts)[None]
    return prefill_out, decode_out


def solution(mesh):
    return jax.shard_map(
        local,
        mesh=mesh,
        in_specs=(
            P("grp", "ctx", None),
            P("grp", "ctx", None),
            P("grp", "ctx", None, None),
            P("grp", "ctx", None),
            P("grp", None, None),
            P("grp", None, None),
            P("grp", "ctx", None),
            P("grp"),
        ),
        out_specs=(P("grp", "ctx", None), P("grp", None, "ctx")),
        check_vma=False,
    )
```

time: 537 us -> 146 us (0.27)
  waiting for transfers between devices: 255 us -> 41.8 us
  matrix products: 89.7 us -> 0 us
  Pallas kernels: 0 us -> 63.1 us
  blocking collectives: 56.1 us -> 0 us
  local copies, waits for them, and re-layouts: 53.6 us -> 8.56 us
  other arithmetic: 32.1 us -> 1.21 us
  loops' own time: 21.2 us -> 0 us
  starting transfers between devices: 13.4 us -> 29.2 us
  between operations: 14.6 us -> 0.78 us
    all_gather x2 -> x0, waiting for transfers between devices: 191 us -> none  [the longest x1 191 us: local(): piece = lax.all_gather(prompt_kv, 'ctx', axis=1, tiled=True)]
    dot_general x24 -> x0, matrix products: 89.7 us -> none  [the longest x8 48.6 us: one_head(): jnp.einsum('cgp,pd->cgd', weights, values, preferred_element_type=jnp.flo...]
    pallas_call x0 -> x6, Pallas kernels: none -> 63.1 us  [the longest x1 30.6 us: prefill(): pl.pallas_call(functools.partial(prefill_kernel, (1024, 1024, 1024, 1408)...]
    all_gather x2 -> x0, blocking collectives: 56.1 us -> none  [merged(): pieces = jax.tree.map(lambda part: lax.all_gather(part, axis), value)]
    all_to_all x2 -> x5, waiting for transfers between devices: 64 us -> 41.8 us  [the longest x1 26.1 us: local(): lax.all_to_all(sent_kv, 'ctx', split_axis=0, concat_axis=0, tiled=True)]
    another operation x2 -> x0, loops' own time: 21.2 us -> none  [the longest x1 21 us: local(): peak, total, mixed = lax.map(one_head, jnp.arange(KVH))]
    reduce_sum x13 -> x0, other arithmetic: 18.8 us -> none  [the longest x8 11.2 us: one_head(): new_total = jnp.sum(weights, axis=-1)]
    while x21 -> x0, local copies, waits for them, and re-layouts: 17.8 us -> none
  transfers between devices with their start and end apart: 4 -> 5, of which waited for: 2 -> 3; matrix products, arithmetic and copies ran while one was open for 7% -> 4% of each run, Pallas kernels for 0% -> 40%
where the time goes in v1:
time: 146 us; the launch traced here: 145 us
  Pallas kernels  63.1 us (43%)
  waiting for transfers between devices  41.8 us (29%)
  starting transfers between devices  29.2 us (20%)
  local copies, waits for them, and re-layouts  8.56 us (6%)
    pallas_call x1, Pallas kernels, prefill(): pl.pallas_call(functools.partial(prefill_kernel, (1024, 1024, 1024, 1408)...  30.6 us
    all_to_all x1, waiting for transfers between devices, local(): lax.all_to_all(sent_kv, 'ctx', split_axis=0, concat_axis=0, tiled=True)  26.1 us
    pallas_call x1, Pallas kernels, blocks(): pl.pallas_call(blocks_kernel, grid=(rows // BLK_ROWS,), in_specs=[pl.Bloc...  11.4 us
    all_to_all x1, waiting for transfers between devices, local(): lax.all_to_all(prefill_parts, 'ctx', split_axis=0, concat_axis=0, tiled=T...  10.6 us
    pallas_call x1, Pallas kernels, query_res(): pl.pallas_call(query_res_kernel, grid=(KVH,), in_specs=[pl.BlockSpec(memo...  7.82 us
    all_to_all x1, starting transfers between devices, local(): lax.all_to_all(spread, 'grp', split_axis=0, concat_axis=0, tiled=True)  7.34 us
    all_to_all x1, starting transfers between devices, local(): lax.all_to_all(sent_kv, 'ctx', split_axis=0, concat_axis=0, tiled=True)  7.04 us
    all_to_all x1, starting transfers between devices, local(): lax.all_to_all(block_parts, 'grp', split_axis=0, concat_axis=0, tiled=True)  6.28 us
  transfers between devices with their start and end apart: 5, of which 3 were waited for; matrix products, arithmetic and copies ran while one was open for 4% of the time, Pallas kernels for 40%

profile of v1, /device:TPU:1, one launch (start us, length us, event | category | flops | bytes accessed | tf_op | source)
XLA Modules:
  0.0 144.7 jit_solution(7434292048891636827)
XLA Ops:
  0.6 1.0 reshape.52
  1.7 0.0 copy-start.5
  1.7 0.8 broadcast_in_dim.17
  2.5 7.3 %all-to-all-start.3 = ((bf16[16,64,128]{2,1,0:T(8,128)(2,1)}), bf16[16,64,128]{2,1,0:T(8,128)(2,1)S(1)}, u32[]{:S(2)}, u32[]{:S(2)}) async-start(bf16[16,64,128]{2,1,0:T(8,128)(2,1)} %broadcast_in_dim.17), calls=%async_computation.3 | async-start | bytes 524288 | tf_op jit(solution)/shard_map/all_to_all | solution.py:329
  9.8 0.7 fusion.3
  10.5 0.1 broadcast_in_dim.14
  10.6 0.1 reshape.55
  10.7 0.6 convert_element_type.10.label_ref
  11.3 6.0 %pack_kv.1 = bf16[8,576,256]{2,1,0:T(8,128)(2,1)} custom-call(bf16[560,2048]{1,0:T(8,128)(2,1)} %bitcast.28, bf16[560,2048]{1,0:T(8,128)(2,1)} %bitcast.29, bf16[16,256]{1,0:T(8,128)(2,1)} %convert_element_type.10.label_ref), custom_call_target="tpu_custom_call" | custom-call | bytes 4600000 | tf_op jit(solution)/shard_map/pack_kv/pallas_call | solution.py:77
  17.3 0.0 copy-start.7
  17.3 0.0 all-to-all-done.3
  17.3 0.0 copy-start.4
  17.3 0.7 copy-done.4
  18.0 7.0 %all-to-all-start.1 = ((bf16[8,576,256]{2,1,0:T(8,128)(2,1)}), bf16[8,576,256]{2,1,0:T(8,128)(2,1)S(1)}, u32[]{:S(2)}, u32[]{:S(2)}) async-start(bf16[8,576,256]{2,1,0:T(8,128)(2,1)} %pack_kv.1), calls=%async_computation.1 | async-start | bytes 4718592 | tf_op jit(solution)/shard_map/all_to_all | solution.py:323
  25.1 0.5 broadcast_subtract_fusion.live_ref
  25.6 7.8 %query_res.1 = bf16[8,592,128]{2,1,0:T(8,128)(2,1)} custom-call(s32[4]{0:T(128)} %broadcast_subtract_fusion.live_ref, bf16[64,8192]{1,0:T(8,128)(2,1)} %bitcast.32, bf16[8,64,128]{2,1,0:T(8,128)(2,1)} %bitcast.34, bf16[4,128,2048]{2,1,0:T(8,128)(2,1)} %v_ref.1, bf16[4,128,2048]{2,1,0:T(8,128)(2,1)} %v_ref.1), custom_call_target="tpu_custom_call" | custom-call | flops 500000000 | bytes 4600000 | tf_op jit(solution)/shard_map/query_res/pallas_call | solution.py:119
  33.4 26.1 %all-to-all-done.1.kv_ref = bf16[8,576,256]{2,1,0:T(8,128)(2,1)S(1)} async-done(((bf16[8,576,256]{2,1,0:T(8,128)(2,1)}), bf16[8,576,256]{2,1,0:T(8,128)(2,1)S(1)}, u32[]{:S(2)}, u32[]{:S(2)}) %all-to-all-start.1) | async-done | bytes 2359328 | tf_op jit(solution)/shard_map/all_to_all | solution.py:323
  59.5 4.3 %all-to-all-start = ((bf16[8,592,128]{2,1,0:T(8,128)(2,1)}), bf16[8,592,128]{2,1,0:T(8,128)(2,1)}, u32[]{:S(2)}, u32[]{:S(2)}) async-start(bf16[8,592,128]{2,1,0:T(8,128)(2,1)} %query_res.1), calls=%async_computation | async-start | bytes 2424832 | tf_op jit(solution)/shard_map/all_to_all | solution.py:332
  63.9 0.7 reshape.61.label_ref
  64.6 11.4 %blocks.1 = bf16[16,80,128]{2,1,0:T(8,128)(2,1)} custom-call(bf16[1024,128]{1,0:T(8,128)(2,1)} %bitcast.35, bf16[4608,256]{1,0:T(8,128)(2,1)} %bitcast.30, s32[1,4608]{1,0:T(1,128)} %reshape.61.label_ref), custom_call_target="tpu_custom_call" | custom-call | flops 8000000000 | bytes 3000000 | tf_op jit(solution)/shard_map/blocks/pallas_call | solution.py:238
  75.9 5.1 %all-to-all-done.q_ref = bf16[8,592,128]{2,1,0:T(8,128)(2,1)} async-done(((bf16[8,592,128]{2,1,0:T(8,128)(2,1)}), bf16[8,592,128]{2,1,0:T(8,128)(2,1)}, u32[]{:S(2)}, u32[]{:S(2)}) %all-to-all-start) | async-done | bytes 1212448 | tf_op jit(solution)/shard_map/all_to_all | solution.py:332
  81.0 6.3 %all-to-all-start.4 = ((bf16[16,80,128]{2,1,0:T(8,128)(2,1)}), bf16[16,80,128]{2,1,0:T(8,128)(2,1)S(1)}, u32[]{:S(2)}, u32[]{:S(2)}) async-start(bf16[16,80,128]{2,1,0:T(8,128)(2,1)} %blocks.1), calls=%async_computation.4 | async-start | bytes 655360 | tf_op jit(solution)/shard_map/all_to_all | solution.py:339
  87.3 30.6 %prefill.1 = bf16[8,64,1024]{2,1,0:T(8,128)(2,1)} custom-call(bf16[8,592,128]{2,1,0:T(8,128)(2,1)} %all-to-all-done.q_ref, bf16[8,576,256]{2,1,0:T(8,128)(2,1)} %copy-done.1), custom_call_target="tpu_custom_call" | custom-call | flops 30000001024 | bytes 5000000 | tf_op jit(solution)/shard_map/prefill/pallas_call | solution.py:179
  117.9 0.0 all-to-all-done.4.blk_ref
  117.9 4.3 %all-to-all-start.2 = ((bf16[8,64,1024]{2,1,0:T(8,128)(2,1)}), bf16[8,64,1024]{2,1,0:T(8,128)(2,1)S(1)}, u32[]{:S(2)}, u32[]{:S(2)}) async-start(bf16[8,64,1024]{2,1,0:T(8,128)(2,1)} %prefill.1), calls=%async_computation.2 | async-start | bytes 2097152 | tf_op jit(solution)/shard_map/all_to_all | solution.py:342
  122.2 0.6 fusion.2
  122.8 1.6 %slice.22.res_ref = bf16[8,80,128]{2,1,0:T(8,128)(2,1)} slice(bf16[8,592,128]{2,1,0:T(8,128)(2,1)} %all-to-all-done.q_ref), slice={[0:8], [512:592], [0:128]} | slice | bytes 327680 | tf_op jit(solution)/shard_map/slice | solution.py:350
  124.4 2.2 %finish.1 = bf16[64,128]{1,0:T(8,128)(2,1)} custom-call(bf16[16,80,128]{2,1,0:T(8,128)(2,1)} %copy-done.2, bf16[8,80,128]{2,1,0:T(8,128)(2,1)} %slice.22.res_ref, bf16[64,128]{1,0:T(8,128)(2,1)} %copy-done.5, bf16[16,128]{1,0:T(8,128)(2,1)} %get-tuple-element.3.nk_ref, bf16[16,128]{1,0:T(8,128)(2,1)} %get-tuple-element.2.nv_ref), custom_call_target="tpu_custom_call" | custom-call | flops 5000000 | bytes 600000 | tf_op jit(solution)/shard_map/finish/pallas_call | solution.py:293
  126.6 1.3 reshape.60
  127.9 10.6 %all-to-all-done.2.in_ref = bf16[8,64,1024]{2,1,0:T(8,128)(2,1)S(1)} async-done(((bf16[8,64,1024]{2,1,0:T(8,128)(2,1)}), bf16[8,64,1024]{2,1,0:T(8,128)(2,1)S(1)}, u32[]{:S(2)}, u32[]{:S(2)}) %all-to-all-start.2) | async-done | bytes 1048608 | tf_op jit(solution)/shard_map/all_to_all | solution.py:342
  138.5 1.0 copy-done
  139.5 5.2 %place.1 = bf16[64,8192]{1,0:T(8,128)(2,1)} custom-call(bf16[8,64,1024]{2,1,0:T(8,128)(2,1)} %copy-done), custom_call_target="tpu_custom_call" | custom-call | bytes 2100000 | tf_op jit(solution)/shard_map/place/pallas_call | solution.py:306
  (20 shorter events, 0.1 us)
Async XLA Ops:
  1.7 15.6 %copy-start.3 = (bf16[8,8,8,128]{3,2,0,1:T(8,128)(2,1)}, bf16[8,8,8,128]{3,2,0,1:T(8,128)(2,1)S(1)}, u32[]{:S(2)}) copy-start(bf16[8,8,8,128]{3,2,0,1:T(8,128)(2,1)S(1)} %copy.18) | copy-start | bytes 393220
  1.7 15.6 %copy-start.5 = (bf16[64,128]{1,0:T(8,128)(2,1)}, bf16[64,128]{1,0:T(8,128)(2,1)S(1)}, u32[]{:S(2)}) copy-start(bf16[64,128]{1,0:T(8,128)(2,1)S(1)} %dynamic-slice_bitcast_fusion.q_ref) | copy-start | bytes 49156
  2.5 14.8 %all-to-all-start.3 = ((bf16[16,64,128]{2,1,0:T(8,128)(2,1)}), bf16[16,64,128]{2,1,0:T(8,128)(2,1)S(1)}, u32[]{:S(2)}, u32[]{:S(2)}) async-start(bf16[16,64,128]{2,1,0:T(8,128)(2,1)} %broadcast_in_dim.17), calls=%async_computation.3 | async-start | bytes 524288 | tf_op jit(solution)/shard_map/all_to_all | solution.py:329
  17.3 7.8 %copy-start.7 = (s32[4]{0:T(128)S(1)}, s32[4]{0:T(128)}, u32[]{:S(2)}) copy-start(s32[4]{0:T(128)} %param.15) | copy-start | bytes 52
  17.3 0.7 copy-start.4
  18.0 41.5 %all-to-all-start.1 = ((bf16[8,576,256]{2,1,0:T(8,128)(2,1)}), bf16[8,576,256]{2,1,0:T(8,128)(2,1)S(1)}, u32[]{:S(2)}, u32[]{:S(2)}) async-start(bf16[8,576,256]{2,1,0:T(8,128)(2,1)} %pack_kv.1), calls=%async_computation.1 | async-start | bytes 4718592 | tf_op jit(solution)/shard_map/all_to_all | solution.py:323
  59.5 5.0 %copy-start.1 = (bf16[8,576,256]{2,1,0:T(8,128)(2,1)}, bf16[8,576,256]{2,1,0:T(8,128)(2,1)S(1)}, u32[]{:S(2)}) copy-start(bf16[8,576,256]{2,1,0:T(8,128)(2,1)S(1)} %all-to-all-done.1.kv_ref) | copy-start | bytes 7077892
  59.5 21.4 %all-to-all-start = ((bf16[8,592,128]{2,1,0:T(8,128)(2,1)}), bf16[8,592,128]{2,1,0:T(8,128)(2,1)}, u32[]{:S(2)}, u32[]{:S(2)}) async-start(bf16[8,592,128]{2,1,0:T(8,128)(2,1)} %query_res.1), calls=%async_computation | async-start | bytes 2424832 | tf_op jit(solution)/shard_map/all_to_all | solution.py:332
  81.0 36.9 %all-to-all-start.4 = ((bf16[16,80,128]{2,1,0:T(8,128)(2,1)}), bf16[16,80,128]{2,1,0:T(8,128)(2,1)S(1)}, u32[]{:S(2)}, u32[]{:S(2)}) async-start(bf16[16,80,128]{2,1,0:T(8,128)(2,1)} %blocks.1), calls=%async_computation.4 | async-start | bytes 655360 | tf_op jit(solution)/shard_map/all_to_all | solution.py:339
  87.3 34.9 %copy-start.6 = (bf16[4,2,2048]{2,1,0:T(2,128)(2,1)S(1)}, bf16[4,2,2048]{2,1,0:T(2,128)(2,1)}, u32[]{:S(2)}) copy-start(bf16[4,2,2048]{2,1,0:T(2,128)(2,1)} %param.13) | copy-start | bytes 98308
  117.9 6.6 %copy-start.2 = (bf16[16,80,128]{2,1,0:T(8,128)(2,1)}, bf16[16,80,128]{2,1,0:T(8,128)(2,1)S(1)}, u32[]{:S(2)}) copy-start(bf16[16,80,128]{2,1,0:T(8,128)(2,1)S(1)} %all-to-all-done.4.blk_ref) | copy-start | bytes 983044
  117.9 20.7 %all-to-all-start.2 = ((bf16[8,64,1024]{2,1,0:T(8,128)(2,1)}), bf16[8,64,1024]{2,1,0:T(8,128)(2,1)S(1)}, u32[]{:S(2)}, u32[]{:S(2)}) async-start(bf16[8,64,1024]{2,1,0:T(8,128)(2,1)} %prefill.1), calls=%async_computation.2 | async-start | bytes 2097152 | tf_op jit(solution)/shard_map/all_to_all | solution.py:342
  138.5 1.0 copy-start

commit v2 on v1

v2 whole, which is shorter than its diff:
```python
import functools
import math

import jax
import jax.numpy as jnp
from jax import lax
from jax.experimental import pallas as pl
from jax.experimental.pallas import tpu as pltpu
from jax.sharding import PartitionSpec as P

HD = 128
KVH = 8
GROUP = 8
PRE_DEV = 496
TAIL_DEV = 64
BLK = 16
ROW_GRP = 4
RES_DEV = 128
KVD = 1024
SEQ_DEV = 560
N_CTX = 8
N_GRP = 16

KEYS = N_CTX * SEQ_DEV
TAIL = N_CTX * TAIL_DEV
Q_ROWS = GROUP * TAIL_DEV
SEND_ROWS = SEQ_DEV + 16
VECS = 2 * GROUP
OWN_VECS = ROW_GRP * VECS
PART_ROWS = OWN_VECS + 16
QPART_ROWS = Q_ROWS + PART_ROWS
STEP = 2
ROWS_STEP = STEP * Q_ROWS
SPAN = 512
REST = SEQ_DEV - SPAN
BITS = (1, 4, 8, 2)

FLOOR = -1e30
LOG2E = 1.4426950408889634
COEF = LOG2E / math.sqrt(HD)
VMEM = 58 * 2**20
NT = (((1,), (1,)), ((), ()))


def widen_query(q):
    scaled = q.astype(jnp.float32) * COEF
    high = scaled.astype(jnp.bfloat16)
    low = (scaled - high.astype(jnp.float32)).astype(jnp.bfloat16)
    return jnp.concatenate([high, low], axis=1)


def part_of(acc, peak):
    rows = acc.shape[0]
    total = jnp.maximum(acc[:, HD:], 1.0)
    out = (acc[:, :HD] / total).astype(jnp.bfloat16)
    weight = peak + jnp.log2(total)
    diag = lax.broadcasted_iota(jnp.int32, (rows, HD), 0) == lax.broadcasted_iota(
        jnp.int32, (rows, HD), 1
    )
    line = jnp.sum(jnp.where(diag, weight, 0.0), axis=0, keepdims=True)
    first = line.astype(jnp.bfloat16)
    rest = line - first.astype(jnp.float32)
    second = rest.astype(jnp.bfloat16)
    third = rest - second.astype(jnp.float32)
    place = lax.broadcasted_iota(jnp.int32, (16, HD), 0)
    stats = jnp.where(
        place == 0,
        first.astype(jnp.float32),
        jnp.where(place == 1, second.astype(jnp.float32), jnp.where(place == 2, third, 0.0)),
    )
    return out, stats.astype(jnp.bfloat16)


def spans(total):
    return [(at, min(SPAN, total - at)) for at in range(0, total, SPAN)]


def whole(space=pltpu.VMEM):
    return pl.BlockSpec(memory_space=space)


def pack_kernel(owner_hbm, row_hbm, kv_ref, out_ref, owner_ref, row_ref, sems, small):
    named = [
        pltpu.make_async_copy(owner_hbm, owner_ref, small.at[0]),
        pltpu.make_async_copy(row_hbm, row_ref, small.at[1]),
    ]
    for copy in named:
        copy.start()
    copies = []

    def add(src, dst):
        copies.append(pltpu.make_async_copy(src, dst, sems.at[len(copies)]))
        copies[-1].start()

    for e in range(KVH):
        for half in range(2):
            lanes = pl.ds(half * HD, HD)
            add(
                kv_ref.at[:, pl.ds(half * KVD + e * HD, HD)],
                out_ref.at[e, pl.ds(0, SEQ_DEV), lanes],
            )
    for copy in named:
        copy.wait()
    shape = (16, 2 * HD)
    place = lax.broadcasted_iota(jnp.int32, shape, 0) * (2 * HD)
    place += lax.broadcasted_iota(jnp.int32, shape, 1)
    rest = place - SPAN - lax.axis_index("ctx") * REST
    rest = jnp.where((rest >= 0) & (rest < REST), rest + SPAN, SEQ_DEV)
    block = jnp.where(place < SPAN, place, rest) // BLK
    labels = jnp.zeros(shape, jnp.float32)
    for b in range(SEQ_DEV // BLK):
        value = (owner_ref[b] * ROW_GRP + row_ref[b]).astype(jnp.float32)
        labels = jnp.where(block == b, value, labels)
    labels = labels.astype(jnp.bfloat16)
    for e in range(KVH):
        out_ref[e, SEQ_DEV:, :] = labels
    for copy in copies:
        copy.wait()


def pack(owner, row, kv):
    return pl.pallas_call(
        pack_kernel,
        in_specs=[whole(pltpu.HBM)] * 3,
        out_specs=whole(),
        out_shape=jax.ShapeDtypeStruct((KVH, SEND_ROWS, 2 * HD), jnp.bfloat16),
        scratch_shapes=[
            pltpu.SMEM((SEQ_DEV // BLK,), jnp.int32),
            pltpu.SMEM((SEQ_DEV // BLK,), jnp.int32),
            pltpu.SemaphoreType.DMA((KVH * 2,)),
            pltpu.SemaphoreType.DMA((2,)),
        ],
        compiler_params=pltpu.CompilerParams(vmem_limit_bytes=VMEM),
        cost_estimate=pl.CostEstimate(flops=0, bytes_accessed=4600000, transcendentals=0),
        name="pack",
    )(owner, row, kv)


def query_res_kernel(live_ref, q_ref, dq_ref, k_ref, v_ref, out_ref, vs_ref):
    for head in range(GROUP):
        out_ref[0, head * TAIL_DEV : (head + 1) * TAIL_DEV, :] = q_ref[
            :, head * HD : (head + 1) * HD
        ]
    keys = k_ref[...].reshape(ROW_GRP * RES_DEV, HD)
    vs_ref[:, :HD] = v_ref[...].reshape(ROW_GRP * RES_DEV, HD)
    vs_ref[:, HD:] = jnp.ones((ROW_GRP * RES_DEV, HD), jnp.bfloat16)
    query = widen_query(dq_ref[0])
    scores = lax.dot_general(query[:, :HD], keys, NT, preferred_element_type=jnp.float32)
    scores += lax.dot_general(query[:, HD:], keys, NT, preferred_element_type=jnp.float32)
    shape = (OWN_VECS, ROW_GRP * RES_DEV)
    row = lax.broadcasted_iota(jnp.int32, shape, 0)
    col = lax.broadcasted_iota(jnp.int32, shape, 1)
    for r in range(ROW_GRP):
        inside = (row >= r * VECS) & (row < (r + 1) * VECS)
        low, high = r * RES_DEV, jnp.clip(live_ref[r], 0, RES_DEV) + r * RES_DEV
        scores = jnp.where(inside & ((col < low) | (col >= high)), -jnp.inf, scores)
    peak = jnp.maximum(jnp.max(scores, axis=1, keepdims=True), FLOOR)
    weights = jnp.exp2(scores - peak).astype(jnp.bfloat16)
    acc = jnp.dot(weights, vs_ref[...], preferred_element_type=jnp.float32)
    out, stats = part_of(acc, peak)
    out_ref[0, Q_ROWS : Q_ROWS + OWN_VECS, :] = out
    out_ref[0, Q_ROWS + OWN_VECS :, :] = stats


def query_res(live, tail_q, dec_vecs, res_kv):
    return pl.pallas_call(
        query_res_kernel,
        grid=(KVH,),
        in_specs=[
            pl.BlockSpec(memory_space=pltpu.SMEM),
            pl.BlockSpec((TAIL_DEV, GROUP * HD), lambda e: (0, e)),
            pl.BlockSpec((1, OWN_VECS, HD), lambda e: (e, 0, 0)),
            pl.BlockSpec((ROW_GRP, RES_DEV, HD), lambda e: (0, 0, e)),
            pl.BlockSpec((ROW_GRP, RES_DEV, HD), lambda e: (0, 0, KVH + e)),
        ],
        out_specs=pl.BlockSpec((1, QPART_ROWS, HD), lambda e: (e, 0, 0)),
        out_shape=jax.ShapeDtypeStruct((KVH, QPART_ROWS, HD), jnp.bfloat16),
        scratch_shapes=[pltpu.VMEM((ROW_GRP * RES_DEV, 2 * HD), jnp.bfloat16)],
        cost_estimate=pl.CostEstimate(flops=500000000, bytes_accessed=4600000, transcendentals=0),
        name="query_res",
    )(live, tail_q, dec_vecs, res_kv, res_kv)


def attend(query, k_s, v_s, pieces, masker, ready=None):
    def score(at, n):
        if ready is not None:
            ready(at)
        scores = lax.dot_general(
            query, k_s[at : at + n, :], NT, preferred_element_type=jnp.float32
        )
        return masker(scores, at)

    peak = acc = None
    scores = score(*pieces[0])
    for i, (at, n) in enumerate(pieces):
        later = score(*pieces[i + 1]) if i + 1 < len(pieces) else None
        top = jnp.maximum(jnp.max(scores, axis=1, keepdims=True), FLOOR)
        new_peak = top if peak is None else jnp.maximum(peak, top)
        weights = jnp.exp2(scores - new_peak).astype(jnp.bfloat16)
        mixed = jnp.dot(weights, v_s[at : at + n, :], preferred_element_type=jnp.float32)
        acc = mixed if peak is None else acc * jnp.exp2(peak - new_peak) + mixed
        peak, scores = new_peak, later
    return peak, acc


def fetch(got_ref, got_s, sems):
    copies = [
        pltpu.make_async_copy(got_ref.at[s], got_s.at[s], sems.at[s]) for s in range(N_CTX)
    ]
    for copy in copies:
        copy.start()
    return copies


def fill(k_s, v_s, at, got_s, shard, src, n):
    keys = got_s[shard, src : src + n, :HD]
    k_s[at : at + n, :HD] = keys
    k_s[at : at + n, HD:] = keys
    v_s[at : at + n, :HD] = got_s[shard, src : src + n, HD:]


def shard_queries(got_ref, step):
    parts = [got_ref[step * STEP + g, :Q_ROWS, :] for g in range(STEP)]
    return widen_query(jnp.concatenate(parts, axis=0))


def blocks_kernel(got_ref, dq_ref, o_ref, k_s, v_s, got_s, sems):
    copies = fetch(got_ref, got_s, sems)
    v_s[:, HD:] = jnp.ones((KEYS, HD), jnp.bfloat16)

    def ready(at):
        first = at // SPAN
        if first < N_CTX:
            copies[first].wait()
            fill(k_s, v_s, at, got_s, first, 0, SPAN)
        else:
            for s in range(N_CTX):
                fill(k_s, v_s, at + s * REST, got_s, s, SPAN, REST)

    rows = dq_ref.shape[0]
    row = lax.broadcasted_iota(jnp.int32, (rows, 1), 0)
    place = row // OWN_VECS
    owner = jnp.zeros_like(place)
    for i, bit in enumerate(BITS):
        owner += (place // 2**i % 2) * bit
    row = (owner * ROW_GRP + row % OWN_VECS // VECS).astype(jnp.float32)

    def labels_of(s, first):
        pair = got_s[s, SEQ_DEV:, :].astype(jnp.float32)
        return jnp.concatenate([pair[first : first + 1], pair[first + 1 : first + 2]], axis=1)

    def masker(scores, at):
        if at // SPAN < N_CTX:
            labels = labels_of(at // SPAN, 0)
        else:
            labels = labels_of(0, 2)
            for s in range(1, N_CTX):
                labels += labels_of(s, 2)
            labels = labels[:, : N_CTX * REST]
        return jnp.where(labels == row, scores, -jnp.inf)

    peak, acc = attend(widen_query(dq_ref[...]), k_s, v_s, spans(KEYS), masker, ready)
    for place in range(rows // OWN_VECS):
        owner = sum((place >> i & 1) * bit for i, bit in enumerate(BITS))
        span = slice(place * OWN_VECS, (place + 1) * OWN_VECS)
        out, stats = part_of(acc[span], peak[span])
        o_ref[owner, :OWN_VECS, :] = out
        o_ref[owner, OWN_VECS:, :] = stats


def blocks(got, dec_vecs):
    return pl.pallas_call(
        blocks_kernel,
        in_specs=[whole(pltpu.HBM), whole()],
        out_specs=whole(),
        out_shape=jax.ShapeDtypeStruct((N_GRP, PART_ROWS, HD), jnp.bfloat16),
        scratch_shapes=[
            pltpu.VMEM((KEYS, 2 * HD), jnp.bfloat16),
            pltpu.VMEM((KEYS, 2 * HD), jnp.bfloat16),
            pltpu.VMEM((N_CTX, SEND_ROWS, 2 * HD), jnp.bfloat16),
            pltpu.SemaphoreType.DMA((N_CTX,)),
        ],
        compiler_params=pltpu.CompilerParams(vmem_limit_bytes=VMEM),
        cost_estimate=pl.CostEstimate(
            flops=8000000000, bytes_accessed=3000000, transcendentals=4700000
        ),
        name="blocks",
    )(got, dec_vecs)


def prefill_kernel(got_q_ref, got_ref, o_ref, k_s, v_s, got_s, sems):
    step = pl.program_id(0)

    @pl.when(step == 0)
    def _():
        copies = fetch(got_ref, got_s, sems)
        v_s[:, HD:] = jnp.ones((KEYS, HD), jnp.bfloat16)
        for s in range(N_CTX):
            copies[s].wait()
            fill(k_s, v_s, s * TAIL_DEV, got_s, s, PRE_DEV, TAIL_DEV)
            fill(k_s, v_s, TAIL + s * PRE_DEV, got_s, s, 0, PRE_DEV)

    def masker(scores, at):
        if at >= TAIL:
            return scores
        row = lax.broadcasted_iota(jnp.int32, (ROWS_STEP, 1), 0)
        token = row % TAIL_DEV + (step * STEP + row // Q_ROWS) * TAIL_DEV
        col = lax.broadcasted_iota(jnp.int32, scores.shape, 1) + at
        return jnp.where(col > token, -jnp.inf, scores)

    _, acc = attend(shard_queries(got_q_ref, step), k_s, v_s, spans(KEYS), masker)
    out = (acc[:, :HD] / acc[:, HD:]).astype(jnp.bfloat16)
    for g in range(STEP):
        for head in range(GROUP):
            at = g * Q_ROWS + head * TAIL_DEV
            o_ref[g, :, head * HD : (head + 1) * HD] = out[at : at + TAIL_DEV]


def prefill(got_q, got):
    return pl.pallas_call(
        prefill_kernel,
        grid=(N_CTX // STEP,),
        in_specs=[whole(), whole(pltpu.HBM)],
        out_specs=pl.BlockSpec((STEP, TAIL_DEV, GROUP * HD), lambda i: (i, 0, 0)),
        out_shape=pltpu.HBM((N_CTX, TAIL_DEV, GROUP * HD), jnp.bfloat16),
        scratch_shapes=[
            pltpu.VMEM((KEYS, 2 * HD), jnp.bfloat16),
            pltpu.VMEM((KEYS, 2 * HD), jnp.bfloat16),
            pltpu.VMEM((N_CTX, SEND_ROWS, 2 * HD), jnp.bfloat16),
            pltpu.SemaphoreType.DMA((N_CTX,)),
        ],
        compiler_params=pltpu.CompilerParams(vmem_limit_bytes=VMEM),
        cost_estimate=pl.CostEstimate(
            flops=26000000000, bytes_accessed=6000000, transcendentals=18000000
        ),
        name="prefill",
    )(got_q, got)


def finish_kernel(blk_ref, in_ref, q_ref, nk_ref, nv_ref, o_ref):
    shape = (OWN_VECS, HD)
    row = lax.broadcasted_iota(jnp.int32, shape, 0)
    col = lax.broadcasted_iota(jnp.int32, shape, 1)
    diag = row == col
    query = widen_query(q_ref[...])
    keys = jnp.concatenate([nk_ref[...], jnp.zeros((HD - 16, HD), jnp.bfloat16)], axis=0)
    values = jnp.concatenate([nv_ref[...], jnp.zeros((HD - 16, HD), jnp.bfloat16)], axis=0)
    scores = lax.dot_general(query[:, :HD], keys, NT, preferred_element_type=jnp.float32)
    scores += lax.dot_general(query[:, HD:], keys, NT, preferred_element_type=jnp.float32)
    open_ = (col // 2 == row // VECS) & (col % 2 <= row % VECS // GROUP)
    scores = jnp.where(open_, scores, -jnp.inf)
    outs, weights = [], []
    parts = [(blk_ref[i, :OWN_VECS, :], blk_ref[i, OWN_VECS:, :]) for i in range(N_GRP)]
    for i in range(N_CTX):
        parts.append(
            (in_ref[i, Q_ROWS : Q_ROWS + OWN_VECS, :], in_ref[i, Q_ROWS + OWN_VECS :, :])
        )
    for out, stats in parts:
        outs.append(out)
        line = jnp.sum(stats.astype(jnp.float32)[:8], axis=0, keepdims=True)
        weights.append(jnp.sum(jnp.where(diag, line, 0.0), axis=1, keepdims=True))
    peak = jnp.max(scores, axis=1, keepdims=True)
    for weight in weights:
        peak = jnp.maximum(peak, weight)
    new = jnp.exp2(scores - peak)
    total = jnp.sum(new, axis=1, keepdims=True)
    mixed = jnp.dot(new.astype(jnp.bfloat16), values, preferred_element_type=jnp.float32)
    for out, weight in zip(outs, weights):
        share = jnp.exp2(weight - peak)
        total += share
        mixed += share * out.astype(jnp.float32)
    out = mixed / total
    for token in range(ROW_GRP * 2):
        for head in range(GROUP):
            at = token * GROUP + head
            o_ref[token : token + 1, head * HD : (head + 1) * HD] = out[at : at + 1].astype(
                jnp.bfloat16
            )


def finish(block_parts, got_q, queries, new_keys, new_values):
    return pl.pallas_call(
        finish_kernel,
        in_specs=[whole()] * 5,
        out_specs=whole(),
        out_shape=jax.ShapeDtypeStruct((ROW_GRP * 2, GROUP * HD), jnp.bfloat16),
        compiler_params=pltpu.CompilerParams(vmem_limit_bytes=16 * 2**20),
        cost_estimate=pl.CostEstimate(flops=5000000, bytes_accessed=1600000, transcendentals=0),
        name="finish",
    )(block_parts, got_q, queries, new_keys, new_values)


def place_kernel(in_ref, out_ref, sems):
    copies = []
    for e in range(KVH):
        lanes = pl.ds(e * GROUP * HD, GROUP * HD)
        copies.append(pltpu.make_async_copy(in_ref.at[e], out_ref.at[:, lanes], sems.at[e]))
        copies[-1].start()
    for copy in copies:
        copy.wait()


def place(parts):
    return pl.pallas_call(
        place_kernel,
        in_specs=[whole()],
        out_specs=whole(pl.ANY),
        out_shape=jax.ShapeDtypeStruct((TAIL_DEV, KVH * GROUP * HD), jnp.bfloat16),
        scratch_shapes=[pltpu.SemaphoreType.DMA((KVH,))],
        compiler_params=pltpu.CompilerParams(vmem_limit_bytes=8 * 2**20),
        cost_estimate=pl.CostEstimate(flops=0, bytes_accessed=2100000, transcendentals=0),
        name="place",
    )(parts)


def spread_over(values, axis, size, before, got):
    values = values + before[0, :1, :] * 0
    me = lax.axis_index(axis)
    for bit in BITS:
        if bit == BITS[-1]:
            values = values + got[0, :1, :HD] * 0
        other = lax.ppermute(values, axis, [(i, i ^ bit) for i in range(size)])
        upper = (me & bit) != 0
        values = jnp.concatenate(
            [jnp.where(upper, other, values), jnp.where(upper, values, other)], axis=0
        )
    return values


def local(tail_q, prompt_kv, dest_owner, dest_row, dec_q, new_kv, res_kv, lens):
    ctx = lax.axis_index("ctx")
    sent = pack(dest_owner.reshape(-1), dest_row.reshape(-1), prompt_kv[0])
    got = lax.all_to_all(sent, "ctx", split_axis=0, concat_axis=0, tiled=True)

    dec_vecs = dec_q.reshape(ROW_GRP * 2, KVH, GROUP, HD).transpose(1, 0, 2, 3)
    dec_vecs = dec_vecs.reshape(KVH, OWN_VECS, HD)
    own_vecs = lax.dynamic_index_in_dim(dec_vecs, ctx, 0, keepdims=False)
    sent_q = query_res(lens - ctx * RES_DEV, tail_q[0], dec_vecs, res_kv)
    got_q = lax.all_to_all(sent_q, "ctx", split_axis=0, concat_axis=0, tiled=True)
    all_vecs = spread_over(own_vecs, "grp", N_GRP, sent_q, got)

    block_parts = blocks(got, all_vecs)
    block_parts = lax.all_to_all(block_parts, "grp", split_axis=0, concat_axis=0, tiled=True)
    parts = prefill(got_q, got)
    parts = lax.all_to_all(parts, "ctx", split_axis=0, concat_axis=0, tiled=True)

    own_new = new_kv.reshape(ROW_GRP * 2, 2, KVH, HD)
    own_new = lax.dynamic_index_in_dim(own_new, ctx, 2, keepdims=False)
    own_new = jnp.pad(own_new, ((0, 8), (0, 0), (0, 0)))
    decode = finish(block_parts, got_q, own_vecs, own_new[:, 0], own_new[:, 1])
    return place(parts)[None], decode.reshape(ROW_GRP, 2, GROUP * HD)


def solution(mesh):
    return jax.shard_map(
        local,
        mesh=mesh,
        in_specs=(
            P("grp", "ctx", None),
            P("grp", "ctx", None),
            P("grp", "ctx", None, None),
            P("grp", "ctx", None),
            P("grp", None, None),
            P("grp", None, None),
            P("grp", "ctx", None),
            P("grp"),
        ),
        out_specs=(P("grp", "ctx", None), P("grp", None, "ctx")),
        check_vma=False,
    )
```

time: 146 us -> 125 us (0.86)
  Pallas kernels: 63.1 us -> 51.2 us
  local copies, waits for them, and re-layouts: 8.56 us -> 2.07 us
  waiting for transfers between devices: 41.8 us -> 38.6 us
  other arithmetic: 1.21 us -> 2.75 us
    pallas_call x5, Pallas kernels: 55.3 us -> 43.4 us  [the longest x1 27.6 us: prefill(): pl.pallas_call(prefill_kernel, grid=(N_CTX // STEP,), in_specs=[whole(),...]
    all_to_all x3 -> x2, waiting for transfers between devices: 36.8 us -> 28.7 us  [the longest x1 14.9 us: local(): lax.all_to_all(parts, 'ctx', split_axis=0, concat_axis=0, tiled=True)]
    ppermute x0 -> x4, starting transfers between devices: none -> 6.14 us  [spread_over(): other = lax.ppermute(values, axis, [(i, i ^ bit) for i in range(size)])]
    all_to_all x3 -> x2, starting transfers between devices: 18.7 us -> 12.8 us  [the longest x1 8.31 us: local(): got = lax.all_to_all(sent, 'ctx', split_axis=0, concat_axis=0, tiled=True)]
    ppermute x0 -> x4, waiting for transfers between devices: none -> 4.6 us  [spread_over(): other = lax.ppermute(values, axis, [(i, i ^ bit) for i in range(size)])]
    slice x1 -> x0, local copies, waits for them, and re-layouts: 1.59 us -> none  [local(): got_q[:, Q_ROWS:, :]]
  transfers between devices with their start and end apart: 5 -> 8, of which waited for: 3 -> 6; matrix products, arithmetic and copies ran while one was open for 4% -> 3% of each run, Pallas kernels for 40% -> 38%
where the time goes in v2:
time: 125 us
  Pallas kernels  51.2 us (41%)
  waiting for transfers between devices  38.6 us (31%)
  starting transfers between devices  29 us (23%)
  other arithmetic  2.75 us (2%)
  local copies, waits for them, and re-layouts  2.07 us (2%)
    pallas_call x1, Pallas kernels, prefill(): pl.pallas_call(prefill_kernel, grid=(N_CTX // STEP,), in_specs=[whole(),...  27.6 us
    all_to_all x1, waiting for transfers between devices, local(): lax.all_to_all(parts, 'ctx', split_axis=0, concat_axis=0, tiled=True)  14.9 us
    all_to_all x1, waiting for transfers between devices, local(): got = lax.all_to_all(sent, 'ctx', split_axis=0, concat_axis=0, tiled=True)  13.7 us
    pallas_call x1, Pallas kernels, blocks(): pl.pallas_call(blocks_kernel, in_specs=[whole(pltpu.HBM), whole()], out_s...  10.9 us
    all_to_all x1, starting transfers between devices, local(): got = lax.all_to_all(sent, 'ctx', split_axis=0, concat_axis=0, tiled=True)  8.31 us
    pallas_call x1, Pallas kernels, query_res(): pl.pallas_call(query_res_kernel, grid=(KVH,), in_specs=[pl.BlockSpec(memo...  7.8 us
    all_to_all x1, starting transfers between devices, local(): lax.all_to_all(block_parts, 'grp', split_axis=0, concat_axis=0, tiled=True)  6.48 us
    ppermute x4, starting transfers between devices, spread_over(): other = lax.ppermute(values, axis, [(i, i ^ bit) for i in range(size)])  6.14 us
  transfers between devices with their start and end apart: 8, of which 6 were waited for; matrix products, arithmetic and copies ran while one was open for 3% of the time, Pallas kernels for 38%

profile of v2, /device:TPU:1, one launch (start us, length us, event | category | flops | bytes accessed | tf_op | source)
XLA Modules:
  0.0 124.6 jit_solution(9976921937329392249)
XLA Ops:
  0.6 3.3 %pack.1 = bf16[8,576,256]{2,1,0:T(8,128)(2,1)} custom-call(s32[35]{0:T(128)} %bitcast.30, s32[35]{0:T(128)} %bitcast.31, bf16[560,2048]{1,0:T(8,128)(2,1)} %bitcast.24), custom_call_target="tpu_custom_call" | custom-call | bytes 4600000 | tf_op jit(solution)/shard_map/pack/pallas_call | solution.py:122
  4.0 0.0 copy-start.3
  4.0 0.0 copy-start.5
  4.0 8.3 %all-to-all-start.1 = ((bf16[8,576,256]{2,1,0:T(8,128)(2,1)}), bf16[8,576,256]{2,1,0:T(8,128)(2,1)S(1)}, u32[]{:S(2)}, u32[]{:S(2)}) async-start(bf16[8,576,256]{2,1,0:T(8,128)(2,1)} %pack.1), calls=%async_computation.1 | async-start | bytes 4718592 | tf_op jit(solution)/shard_map/all_to_all | solution.py:433
  12.3 0.1 reshape.40
  12.4 0.7 copy.15
  13.1 0.5 broadcast_subtract_fusion.live_ref
  13.6 7.8 %query_res.1 = bf16[8,592,128]{2,1,0:T(8,128)(2,1)} custom-call(s32[4]{0:T(128)} %broadcast_subtract_fusion.live_ref, bf16[64,8192]{1,0:T(8,128)(2,1)} %bitcast.26, bf16[8,64,128]{2,1,0:T(8,128)(2,1)} %bitcast.27, bf16[4,128,2048]{2,1,0:T(8,128)(2,1)} %v_ref.1, bf16[4,128,2048]{2,1,0:T(8,128)(2,1)} %v_ref.1), custom_call_target="tpu_custom_call" | custom-call | flops 500000000 | bytes 4600000 | tf_op jit(solution)/shard_map/query_res/pallas_call | solution.py:166
  21.4 0.7 fusion.3
  22.1 0.7 broadcast_add_fusion
  22.8 1.0 collective-permute-start
  23.8 0.8 collective-permute-done
  24.6 1.4 %collective-permute-start.1 = (bf16[128,128]{1,0:T(8,128)(2,1)S(1)}, bf16[128,128]{1,0:T(8,128)(2,1)S(1)}, u32[]{:S(2)}, u32[]{:S(2)}) collective-permute-start(bf16[128,128]{1,0:T(8,128)(2,1)S(1)} %pad_maximum_fusion.2), channel_id=1, source_target_pairs={{0,4},{1,5},{2,6},{3,7},{4,0},{5,1},{6,2},{7,3},{8,12},{9,13},{10,... | collective-permute-start | bytes 98312 | tf_op jit(solution)/shard_map/ppermute | solution.py:422
  26.0 1.8 %collective-permute-done.1 = bf16[128,128]{1,0:T(8,128)(2,1)S(1)} collective-permute-done((bf16[128,128]{1,0:T(8,128)(2,1)S(1)}, bf16[128,128]{1,0:T(8,128)(2,1)S(1)}, u32[]{:S(2)}, u32[]{:S(2)}) %collective-permute-start.1) | collective-permute-done | bytes 32800 | tf_op jit(solution)/shard_map/ppermute | solution.py:422
  27.8 3.0 %collective-permute-start.2 = (bf16[256,128]{1,0:T(8,128)(2,1)S(1)}, bf16[256,128]{1,0:T(8,128)(2,1)S(1)}, u32[]{:S(2)}, u32[]{:S(2)}) collective-permute-start(bf16[256,128]{1,0:T(8,128)(2,1)S(1)} %pad_maximum_fusion.1), channel_id=1, source_target_pairs={{0,8},{1,9},{2,10},{3,11},{4,12},{5,13},{6,14},{7,15},{8,0},{9,1},... | collective-permute-start | bytes 196616 | tf_op jit(solution)/shard_map/ppermute | solution.py:422
  30.8 2.0 %collective-permute-done.2 = bf16[256,128]{1,0:T(8,128)(2,1)S(1)} collective-permute-done((bf16[256,128]{1,0:T(8,128)(2,1)S(1)}, bf16[256,128]{1,0:T(8,128)(2,1)S(1)}, u32[]{:S(2)}, u32[]{:S(2)}) %collective-permute-start.2) | collective-permute-done | bytes 65568 | tf_op jit(solution)/shard_map/ppermute | solution.py:422
  32.8 13.7 %all-to-all-done.1.got_ref = bf16[8,576,256]{2,1,0:T(8,128)(2,1)S(1)} async-done(((bf16[8,576,256]{2,1,0:T(8,128)(2,1)}), bf16[8,576,256]{2,1,0:T(8,128)(2,1)S(1)}, u32[]{:S(2)}, u32[]{:S(2)}) %all-to-all-start.1) | async-done | bytes 2359328 | tf_op jit(solution)/shard_map/all_to_all | solution.py:433
  46.6 0.8 collective-permute-start.3
  47.4 0.6 copy-done.2
  48.0 3.6 %all-to-all-start = ((bf16[8,592,128]{2,1,0:T(8,128)(2,1)}), bf16[8,592,128]{2,1,0:T(8,128)(2,1)S(1)}, u32[]{:S(2)}, u32[]{:S(2)}) async-start(bf16[8,592,128]{2,1,0:T(8,128)(2,1)} %query_res.1), calls=%async_computation | async-start | bytes 2424832 | tf_op jit(solution)/shard_map/all_to_all | solution.py:439
  51.5 0.0 collective-permute-done.3
  51.6 0.7 pad_maximum_fusion.dq_ref
  52.3 10.9 %blocks.1 = bf16[16,80,128]{2,1,0:T(8,128)(2,1)} custom-call(bf16[8,576,256]{2,1,0:T(8,128)(2,1)} %copy-done.2, bf16[1024,128]{1,0:T(8,128)(2,1)} %pad_maximum_fusion.dq_ref), custom_call_target="tpu_custom_call" | custom-call | flops 8000000000 | bytes 3000000 | tf_op jit(solution)/shard_map/blocks/pallas_call | solution.py:272
  63.2 5.4 %all-to-all-done.got_q_ref.in_ref = bf16[8,592,128]{2,1,0:T(8,128)(2,1)S(1)} async-done(((bf16[8,592,128]{2,1,0:T(8,128)(2,1)}), bf16[8,592,128]{2,1,0:T(8,128)(2,1)S(1)}, u32[]{:S(2)}, u32[]{:S(2)}) %all-to-all-start) | async-done | bytes 1212448 | tf_op jit(solution)/shard_map/all_to_all | solution.py:439
  68.6 6.5 %all-to-all-start.3 = ((bf16[16,80,128]{2,1,0:T(8,128)(2,1)}), bf16[16,80,128]{2,1,0:T(8,128)(2,1)S(1)}, u32[]{:S(2)}, u32[]{:S(2)}) async-start(bf16[16,80,128]{2,1,0:T(8,128)(2,1)} %blocks.1), calls=%async_computation.3 | async-start | bytes 655360 | tf_op jit(solution)/shard_map/all_to_all | solution.py:443
  75.0 0.0 copy-start.4
  75.1 27.6 %prefill.1 = bf16[8,64,1024]{2,1,0:T(8,128)(2,1)} custom-call(bf16[8,592,128]{2,1,0:T(8,128)(2,1)} %copy-done, bf16[8,576,256]{2,1,0:T(8,128)(2,1)} %copy-done.2), custom_call_target="tpu_custom_call" | custom-call | flops 25999998976 | bytes 6000000 | tf_op jit(solution)/shard_map/prefill/pallas_call | solution.py:320
  102.7 4.5 %all-to-all-start.2 = ((bf16[8,64,1024]{2,1,0:T(8,128)(2,1)}), bf16[8,64,1024]{2,1,0:T(8,128)(2,1)S(1)}, u32[]{:S(2)}, u32[]{:S(2)}) async-start(bf16[8,64,1024]{2,1,0:T(8,128)(2,1)} %prefill.1), calls=%async_computation.2 | async-start | bytes 2097152 | tf_op jit(solution)/shard_map/all_to_all | solution.py:445
  107.3 0.5 finish.1
  107.8 0.6 reshape.45
  108.4 14.9 %all-to-all-done.2.in_ref = bf16[8,64,1024]{2,1,0:T(8,128)(2,1)S(1)} async-done(((bf16[8,64,1024]{2,1,0:T(8,128)(2,1)}), bf16[8,64,1024]{2,1,0:T(8,128)(2,1)S(1)}, u32[]{:S(2)}, u32[]{:S(2)}) %all-to-all-start.2) | async-done | bytes 1048608 | tf_op jit(solution)/shard_map/all_to_all | solution.py:445
  123.4 1.0 place.1
  (21 shorter events, 0.2 us)
Async XLA Ops:
  4.0 8.3 %copy-start.3 = (bf16[4,2,8192]{2,1,0:T(2,128)(2,1)S(1)}, bf16[4,2,8192]{2,1,0:T(2,128)(2,1)}, u32[]{:S(2)}) copy-start(bf16[4,2,8192]{2,1,0:T(2,128)(2,1)} %param.12) | copy-start | bytes 393220
  4.0 9.1 %copy-start.5 = (s32[4]{0:T(128)S(1)}, s32[4]{0:T(128)}, u32[]{:S(2)}) copy-start(s32[4]{0:T(128)} %param.15) | copy-start | bytes 52
  4.0 42.5 %all-to-all-start.1 = ((bf16[8,576,256]{2,1,0:T(8,128)(2,1)}), bf16[8,576,256]{2,1,0:T(8,128)(2,1)S(1)}, u32[]{:S(2)}, u32[]{:S(2)}) async-start(bf16[8,576,256]{2,1,0:T(8,128)(2,1)} %pack.1), calls=%async_computation.1 | async-start | bytes 4718592 | tf_op jit(solution)/shard_map/all_to_all | solution.py:433
  22.8 1.8 %collective-permute-start = (bf16[64,128]{1,0:T(8,128)(2,1)S(1)}, bf16[64,128]{1,0:T(8,128)(2,1)S(1)}, u32[]{:S(2)}, u32[]{:S(2)}) collective-permute-start(bf16[64,128]{1,0:T(8,128)(2,1)S(1)} %get-tuple-element.2), channel_id=1, source_target_pairs={{0,1},{1,0},{2,3},{3,2},{4,5},{5,4},{6,7},{7,6},{8,9},{9,8},{10,11... | collective-permute-start | bytes 49160 | tf_op jit(solution)/shard_map/ppermute | solution.py:422
  24.6 3.1 %collective-permute-start.1 = (bf16[128,128]{1,0:T(8,128)(2,1)S(1)}, bf16[128,128]{1,0:T(8,128)(2,1)S(1)}, u32[]{:S(2)}, u32[]{:S(2)}) collective-permute-start(bf16[128,128]{1,0:T(8,128)(2,1)S(1)} %pad_maximum_fusion.2), channel_id=1, source_target_pairs={{0,4},{1,5},{2,6},{3,7},{4,0},{5,1},{6,2},{7,3},{8,12},{9,13},{10,... | collective-permute-start | bytes 98312 | tf_op jit(solution)/shard_map/ppermute | solution.py:422
  27.8 5.0 %collective-permute-start.2 = (bf16[256,128]{1,0:T(8,128)(2,1)S(1)}, bf16[256,128]{1,0:T(8,128)(2,1)S(1)}, u32[]{:S(2)}, u32[]{:S(2)}) collective-permute-start(bf16[256,128]{1,0:T(8,128)(2,1)S(1)} %pad_maximum_fusion.1), channel_id=1, source_target_pairs={{0,8},{1,9},{2,10},{3,11},{4,12},{5,13},{6,14},{7,15},{8,0},{9,1},... | collective-permute-start | bytes 196616 | tf_op jit(solution)/shard_map/ppermute | solution.py:422
  46.5 1.4 %copy-start.2 = (bf16[8,576,256]{2,1,0:T(8,128)(2,1)}, bf16[8,576,256]{2,1,0:T(8,128)(2,1)S(1)}, u32[]{:S(2)}) copy-start(bf16[8,576,256]{2,1,0:T(8,128)(2,1)S(1)} %all-to-all-done.1.got_ref) | copy-start | bytes 7077892
  46.6 5.0 %collective-permute-start.3 = (bf16[512,128]{1,0:T(8,128)(2,1)S(1)}, bf16[512,128]{1,0:T(8,128)(2,1)S(1)}, u32[]{:S(2)}, u32[]{:S(2)}) collective-permute-start(bf16[512,128]{1,0:T(8,128)(2,1)S(1)} %maximum_add_fusion), channel_id=1, source_target_pairs={{0,2},{1,3},{2,0},{3,1},{4,6},{5,7},{6,4},{7,5},{8,10},{9,11},{10,... | collective-permute-start | bytes 393224 | tf_op jit(solution)/shard_map/ppermute | solution.py:422
  48.0 20.6 %all-to-all-start = ((bf16[8,592,128]{2,1,0:T(8,128)(2,1)}), bf16[8,592,128]{2,1,0:T(8,128)(2,1)S(1)}, u32[]{:S(2)}, u32[]{:S(2)}) async-start(bf16[8,592,128]{2,1,0:T(8,128)(2,1)} %query_res.1), calls=%async_computation | async-start | bytes 2424832 | tf_op jit(solution)/shard_map/all_to_all | solution.py:439
  68.6 6.5 %copy-start = (bf16[8,592,128]{2,1,0:T(8,128)(2,1)}, bf16[8,592,128]{2,1,0:T(8,128)(2,1)S(1)}, u32[]{:S(2)}) copy-start(bf16[8,592,128]{2,1,0:T(8,128)(2,1)S(1)} %all-to-all-done.got_q_ref.in_ref) | copy-start | bytes 3637252
  68.6 34.1 %all-to-all-start.3 = ((bf16[16,80,128]{2,1,0:T(8,128)(2,1)}), bf16[16,80,128]{2,1,0:T(8,128)(2,1)S(1)}, u32[]{:S(2)}, u32[]{:S(2)}) async-start(bf16[16,80,128]{2,1,0:T(8,128)(2,1)} %blocks.1), calls=%async_computation.3 | async-start | bytes 655360 | tf_op jit(solution)/shard_map/all_to_all | solution.py:443
  75.0 32.2 %copy-start.4 = (bf16[4,2,2048]{2,1,0:T(2,128)(2,1)S(1)}, bf16[4,2,2048]{2,1,0:T(2,128)(2,1)}, u32[]{:S(2)}) copy-start(bf16[4,2,2048]{2,1,0:T(2,128)(2,1)} %param.13) | copy-start | bytes 98308
  102.7 4.6 %copy-start.1 = (bf16[8,592,128]{2,1,0:T(8,128)(2,1)S(1)}, bf16[8,592,128]{2,1,0:T(8,128)(2,1)}, u32[]{:S(2)}) copy-start(bf16[8,592,128]{2,1,0:T(8,128)(2,1)} %copy-done) | copy-start | bytes 3637252
  102.7 20.7 %all-to-all-start.2 = ((bf16[8,64,1024]{2,1,0:T(8,128)(2,1)}), bf16[8,64,1024]{2,1,0:T(8,128)(2,1)S(1)}, u32[]{:S(2)}, u32[]{:S(2)}) async-start(bf16[8,64,1024]{2,1,0:T(8,128)(2,1)} %prefill.1), calls=%async_computation.2 | async-start | bytes 2097152 | tf_op jit(solution)/shard_map/all_to_all | solution.py:445

commit v3 on v2

--- a/solution.py
+++ b/solution.py
@@ -79,7 +79,9 @@
     return pl.BlockSpec(memory_space=space)
 
 
-def pack_kernel(owner_hbm, row_hbm, kv_ref, out_ref, owner_ref, row_ref, sems, small):
+def pack_kernel(
+    owner_hbm, row_hbm, kv_ref, out_hbm, out_ref, owner_ref, row_ref, sems, small, done
+):
     named = [
         pltpu.make_async_copy(owner_hbm, owner_ref, small.at[0]),
         pltpu.make_async_copy(row_hbm, row_ref, small.at[1]),
@@ -114,7 +116,13 @@
     labels = labels.astype(jnp.bfloat16)
     for e in range(KVH):
         out_ref[e, SEQ_DEV:, :] = labels
-    for copy in copies:
+    written = []
+    for e in range(KVH):
+        copies[2 * e].wait()
+        copies[2 * e + 1].wait()
+        written.append(pltpu.make_async_copy(out_ref.at[e], out_hbm.at[e], done.at[e]))
+        written[-1].start()
+    for copy in written:
         copy.wait()
 
 
@@ -122,13 +130,15 @@
     return pl.pallas_call(
         pack_kernel,
         in_specs=[whole(pltpu.HBM)] * 3,
-        out_specs=whole(),
+        out_specs=whole(pltpu.HBM),
         out_shape=jax.ShapeDtypeStruct((KVH, SEND_ROWS, 2 * HD), jnp.bfloat16),
         scratch_shapes=[
+            pltpu.VMEM((KVH, SEND_ROWS, 2 * HD), jnp.bfloat16),
             pltpu.SMEM((SEQ_DEV // BLK,), jnp.int32),
             pltpu.SMEM((SEQ_DEV // BLK,), jnp.int32),
             pltpu.SemaphoreType.DMA((KVH * 2,)),
             pltpu.SemaphoreType.DMA((2,)),
+            pltpu.SemaphoreType.DMA((KVH,)),
         ],
         compiler_params=pltpu.CompilerParams(vmem_limit_bytes=VMEM),
         cost_estimate=pl.CostEstimate(flops=0, bytes_accessed=4600000, transcendentals=0),
@@ -272,11 +282,13 @@
     return pl.pallas_call(
         blocks_kernel,
         in_specs=[whole(pltpu.HBM), whole()],
-        out_specs=whole(),
-        out_shape=jax.ShapeDtypeStruct((N_GRP, PART_ROWS, HD), jnp.bfloat16),
+        out_specs=[whole()] * 3,
+        out_shape=[
+            jax.ShapeDtypeStruct((N_GRP, PART_ROWS, HD), jnp.bfloat16),
+            jax.ShapeDtypeStruct((KEYS, 2 * HD), jnp.bfloat16),
+            jax.ShapeDtypeStruct((KEYS, 2 * HD), jnp.bfloat16),
+        ],
         scratch_shapes=[
-            pltpu.VMEM((KEYS, 2 * HD), jnp.bfloat16),
-            pltpu.VMEM((KEYS, 2 * HD), jnp.bfloat16),
             pltpu.VMEM((N_CTX, SEND_ROWS, 2 * HD), jnp.bfloat16),
             pltpu.SemaphoreType.DMA((N_CTX,)),
         ],
@@ -288,27 +300,23 @@
     )(got, dec_vecs)
 
 
-def prefill_kernel(got_q_ref, got_ref, o_ref, k_s, v_s, got_s, sems):
+def prefill_kernel(got_q_ref, k_s, v_s, o_ref):
     step = pl.program_id(0)
-
-    @pl.when(step == 0)
-    def _():
-        copies = fetch(got_ref, got_s, sems)
-        v_s[:, HD:] = jnp.ones((KEYS, HD), jnp.bfloat16)
-        for s in range(N_CTX):
-            copies[s].wait()
-            fill(k_s, v_s, s * TAIL_DEV, got_s, s, PRE_DEV, TAIL_DEV)
-            fill(k_s, v_s, TAIL + s * PRE_DEV, got_s, s, 0, PRE_DEV)
+    row = lax.broadcasted_iota(jnp.int32, (ROWS_STEP, 1), 0)
+    token = row % TAIL_DEV + (step * STEP + row // Q_ROWS) * TAIL_DEV
 
     def masker(scores, at):
-        if at >= TAIL:
-            return scores
-        row = lax.broadcasted_iota(jnp.int32, (ROWS_STEP, 1), 0)
-        token = row % TAIL_DEV + (step * STEP + row // Q_ROWS) * TAIL_DEV
-        col = lax.broadcasted_iota(jnp.int32, scores.shape, 1) + at
-        return jnp.where(col > token, -jnp.inf, scores)
-
-    _, acc = attend(shard_queries(got_q_ref, step), k_s, v_s, spans(KEYS), masker)
+        shard = at // SPAN
+        if shard < N_CTX:
+            col = lax.broadcasted_iota(jnp.int32, (1, HD), 1) - (HD - SPAN + PRE_DEV)
+            place = jnp.where(col >= 0, col + shard * TAIL_DEV, -1)
+            last = jnp.where(place > token, -jnp.inf, scores[:, SPAN - HD :])
+            return jnp.concatenate([scores[:, : SPAN - HD], last], axis=1)
+        col = lax.broadcasted_iota(jnp.int32, (1, N_CTX * REST), 1)
+        place = col // REST * TAIL_DEV + (SPAN - PRE_DEV) + col % REST
+        return jnp.where(place > token, -jnp.inf, scores)
+
+    _, acc = attend(shard_queries(got_q_ref, 0), k_s, v_s, spans(KEYS), masker)
     out = (acc[:, :HD] / acc[:, HD:]).astype(jnp.bfloat16)
     for g in range(STEP):
         for head in range(GROUP):
@@ -316,25 +324,23 @@
             o_ref[g, :, head * HD : (head + 1) * HD] = out[at : at + TAIL_DEV]
 
 
-def prefill(got_q, got):
+def prefill(got_q, keys, values):
     return pl.pallas_call(
         prefill_kernel,
         grid=(N_CTX // STEP,),
-        in_specs=[whole(), whole(pltpu.HBM)],
+        in_specs=[
+            pl.BlockSpec((STEP, QPART_ROWS, HD), lambda i: (i, 0, 0)),
+            whole(),
+            whole(),
+        ],
         out_specs=pl.BlockSpec((STEP, TAIL_DEV, GROUP * HD), lambda i: (i, 0, 0)),
-        out_shape=pltpu.HBM((N_CTX, TAIL_DEV, GROUP * HD), jnp.bfloat16),
-        scratch_shapes=[
-            pltpu.VMEM((KEYS, 2 * HD), jnp.bfloat16),
-            pltpu.VMEM((KEYS, 2 * HD), jnp.bfloat16),
-            pltpu.VMEM((N_CTX, SEND_ROWS, 2 * HD), jnp.bfloat16),
-            pltpu.SemaphoreType.DMA((N_CTX,)),
-        ],
+        out_shape=jax.ShapeDtypeStruct((N_CTX, TAIL_DEV, GROUP * HD), jnp.bfloat16),
         compiler_params=pltpu.CompilerParams(vmem_limit_bytes=VMEM),
         cost_estimate=pl.CostEstimate(
             flops=26000000000, bytes_accessed=6000000, transcendentals=18000000
         ),
         name="prefill",
-    )(got_q, got)
+    )(got_q, keys, values)
 
 
 def finish_kernel(blk_ref, in_ref, q_ref, nk_ref, nv_ref, o_ref):
@@ -439,9 +445,9 @@
     got_q = lax.all_to_all(sent_q, "ctx", split_axis=0, concat_axis=0, tiled=True)
     all_vecs = spread_over(own_vecs, "grp", N_GRP, sent_q, got)
 
-    block_parts = blocks(got, all_vecs)
+    block_parts, keys, values = blocks(got, all_vecs)
     block_parts = lax.all_to_all(block_parts, "grp", split_axis=0, concat_axis=0, tiled=True)
-    parts = prefill(got_q, got)
+    parts = prefill(got_q, keys, values)
     parts = lax.all_to_all(parts, "ctx", split_axis=0, concat_axis=0, tiled=True)
 
     own_new = new_kv.reshape(ROW_GRP * 2, 2, KVH, HD)

time: 125 us -> 123 us (0.984)
  Pallas kernels: 51.2 us -> 49.2 us
    pallas_call x1, Pallas kernels: 27.6 us -> 26.1 us  [prefill(): pl.pallas_call(prefill_kernel, grid=(N_CTX // STEP,), in_specs=[pl.BlockS...]
  transfers between devices with their start and end apart: 8 -> 8, of which waited for: 6 -> 6; matrix products, arithmetic and copies ran while one was open for 3% -> 3% of each run, Pallas kernels for 38% -> 37%
where the time goes in v3:
time: 123 us
  Pallas kernels  49.2 us (40%)
  waiting for transfers between devices  38.6 us (31%)
  starting transfers between devices  29 us (24%)
  other arithmetic  2.76 us (2%)
  local copies, waits for them, and re-layouts  2.07 us (2%)
    pallas_call x1, Pallas kernels, prefill(): pl.pallas_call(prefill_kernel, grid=(N_CTX // STEP,), in_specs=[pl.BlockS...  26.1 us
    all_to_all x1, waiting for transfers between devices, local(): lax.all_to_all(parts, 'ctx', split_axis=0, concat_axis=0, tiled=True)  15.1 us
    all_to_all x1, waiting for transfers between devices, local(): got = lax.all_to_all(sent, 'ctx', split_axis=0, concat_axis=0, tiled=True)  13.7 us
    pallas_call x1, Pallas kernels, blocks(): pl.pallas_call(blocks_kernel, in_specs=[whole(pltpu.HBM), whole()], out_s...  11 us
    all_to_all x1, starting transfers between devices, local(): got = lax.all_to_all(sent, 'ctx', split_axis=0, concat_axis=0, tiled=True)  8.31 us
    pallas_call x1, Pallas kernels, query_res(): pl.pallas_call(query_res_kernel, grid=(KVH,), in_specs=[pl.BlockSpec(memo...  7.83 us
    all_to_all x1, starting transfers between devices, local(): lax.all_to_all(block_parts, 'grp', split_axis=0, concat_axis=0, tiled=True)  6.48 us
    ppermute x4, starting transfers between devices, spread_over(): other = lax.ppermute(values, axis, [(i, i ^ bit) for i in range(size)])  6.14 us
  transfers between devices with their start and end apart: 8, of which 6 were waited for; matrix products, arithmetic and copies ran while one was open for 3% of the time, Pallas kernels for 37%

profile of v3, /device:TPU:1, one launch (start us, length us, event | category | flops | bytes accessed | tf_op | source)
XLA Modules:
  0.0 122.6 jit_solution(5396342572279454559)
XLA Ops:
  0.6 2.7 %pack.1 = bf16[8,576,256]{2,1,0:T(8,128)(2,1)} custom-call(s32[35]{0:T(128)} %bitcast.30, s32[35]{0:T(128)} %bitcast.31, bf16[560,2048]{1,0:T(8,128)(2,1)} %bitcast.24), custom_call_target="tpu_custom_call" | custom-call | bytes 4600000 | tf_op jit(solution)/shard_map/pack/pallas_call | solution.py:130
  3.4 0.0 copy-start.3
  3.4 0.0 copy-start.5
  3.4 8.3 %all-to-all-start.1 = ((bf16[8,576,256]{2,1,0:T(8,128)(2,1)}), bf16[8,576,256]{2,1,0:T(8,128)(2,1)S(1)}, u32[]{:S(2)}, u32[]{:S(2)}) async-start(bf16[8,576,256]{2,1,0:T(8,128)(2,1)} %pack.1), calls=%async_computation.1 | async-start | bytes 4718592 | tf_op jit(solution)/shard_map/all_to_all | solution.py:439
  11.7 0.1 reshape.40
  11.8 0.7 copy.15
  12.5 0.5 broadcast_subtract_fusion.live_ref
  13.0 7.8 %query_res.1 = bf16[8,592,128]{2,1,0:T(8,128)(2,1)} custom-call(s32[4]{0:T(128)} %broadcast_subtract_fusion.live_ref, bf16[64,8192]{1,0:T(8,128)(2,1)} %bitcast.26, bf16[8,64,128]{2,1,0:T(8,128)(2,1)} %bitcast.27, bf16[4,128,2048]{2,1,0:T(8,128)(2,1)} %v_ref.1, bf16[4,128,2048]{2,1,0:T(8,128)(2,1)} %v_ref.1), custom_call_target="tpu_custom_call" | custom-call | flops 500000000 | bytes 4600000 | tf_op jit(solution)/shard_map/query_res/pallas_call | solution.py:176
  20.9 0.7 fusion.3
  21.5 0.7 broadcast_add_fusion
  22.3 1.0 collective-permute-start
  23.2 0.8 collective-permute-done
  24.1 1.4 %collective-permute-start.1 = (bf16[128,128]{1,0:T(8,128)(2,1)S(1)}, bf16[128,128]{1,0:T(8,128)(2,1)S(1)}, u32[]{:S(2)}, u32[]{:S(2)}) collective-permute-start(bf16[128,128]{1,0:T(8,128)(2,1)S(1)} %pad_maximum_fusion.2), channel_id=1, source_target_pairs={{0,4},{1,5},{2,6},{3,7},{4,0},{5,1},{6,2},{7,3},{8,12},{9,13},{10,... | collective-permute-start | bytes 98312 | tf_op jit(solution)/shard_map/ppermute | solution.py:428
  25.4 1.8 %collective-permute-done.1 = bf16[128,128]{1,0:T(8,128)(2,1)S(1)} collective-permute-done((bf16[128,128]{1,0:T(8,128)(2,1)S(1)}, bf16[128,128]{1,0:T(8,128)(2,1)S(1)}, u32[]{:S(2)}, u32[]{:S(2)}) %collective-permute-start.1) | collective-permute-done | bytes 32800 | tf_op jit(solution)/shard_map/ppermute | solution.py:428
  27.2 3.0 %collective-permute-start.2 = (bf16[256,128]{1,0:T(8,128)(2,1)S(1)}, bf16[256,128]{1,0:T(8,128)(2,1)S(1)}, u32[]{:S(2)}, u32[]{:S(2)}) collective-permute-start(bf16[256,128]{1,0:T(8,128)(2,1)S(1)} %pad_maximum_fusion.1), channel_id=1, source_target_pairs={{0,8},{1,9},{2,10},{3,11},{4,12},{5,13},{6,14},{7,15},{8,0},{9,1},... | collective-permute-start | bytes 196616 | tf_op jit(solution)/shard_map/ppermute | solution.py:428
  30.2 2.0 %collective-permute-done.2 = bf16[256,128]{1,0:T(8,128)(2,1)S(1)} collective-permute-done((bf16[256,128]{1,0:T(8,128)(2,1)S(1)}, bf16[256,128]{1,0:T(8,128)(2,1)S(1)}, u32[]{:S(2)}, u32[]{:S(2)}) %collective-permute-start.2) | collective-permute-done | bytes 65568 | tf_op jit(solution)/shard_map/ppermute | solution.py:428
  32.3 13.7 %all-to-all-done.1.got_ref = bf16[8,576,256]{2,1,0:T(8,128)(2,1)S(1)} async-done(((bf16[8,576,256]{2,1,0:T(8,128)(2,1)}), bf16[8,576,256]{2,1,0:T(8,128)(2,1)S(1)}, u32[]{:S(2)}, u32[]{:S(2)}) %all-to-all-start.1) | async-done | bytes 2359328 | tf_op jit(solution)/shard_map/all_to_all | solution.py:439
  46.0 0.8 collective-permute-start.3
  46.8 0.6 copy-done.2
  47.4 3.6 %all-to-all-start = ((bf16[8,592,128]{2,1,0:T(8,128)(2,1)}), bf16[8,592,128]{2,1,0:T(8,128)(2,1)S(1)}, u32[]{:S(2)}, u32[]{:S(2)}) async-start(bf16[8,592,128]{2,1,0:T(8,128)(2,1)} %query_res.1), calls=%async_computation | async-start | bytes 2424832 | tf_op jit(solution)/shard_map/all_to_all | solution.py:445
  50.9 0.0 collective-permute-done.3
  51.0 0.7 pad_maximum_fusion.dq_ref
  51.7 11.0 %blocks.1 = (bf16[16,80,128]{2,1,0:T(8,128)(2,1)}, bf16[4480,256]{1,0:T(8,128)(2,1)}, bf16[4480,256]{1,0:T(8,128)(2,1)}) custom-call(bf16[8,576,256]{2,1,0:T(8,128)(2,1)} %copy-done.2, bf16[1024,128]{1,0:T(8,128)(2,1)} %pad_maximum_fusion.dq_ref), custom_call_target="tpu_custom_call" | custom-call | flops 8000000000 | bytes 3000000 | tf_op jit(solution)/shard_map/blocks/pallas_call | solution.py:282
  62.7 5.2 %all-to-all-done.got_q_ref.in_ref = bf16[8,592,128]{2,1,0:T(8,128)(2,1)S(1)} async-done(((bf16[8,592,128]{2,1,0:T(8,128)(2,1)}), bf16[8,592,128]{2,1,0:T(8,128)(2,1)S(1)}, u32[]{:S(2)}, u32[]{:S(2)}) %all-to-all-start) | async-done | bytes 1212448 | tf_op jit(solution)/shard_map/all_to_all | solution.py:445
  68.0 6.5 %all-to-all-start.3 = ((bf16[16,80,128]{2,1,0:T(8,128)(2,1)}), bf16[16,80,128]{2,1,0:T(8,128)(2,1)S(1)}, u32[]{:S(2)}, u32[]{:S(2)}) async-start(bf16[16,80,128]{2,1,0:T(8,128)(2,1)} %get-tuple-element.7), calls=%async_computation.3 | async-start | bytes 655360 | tf_op jit(solution)/shard_map/all_to_all | solution.py:449
  74.4 0.0 copy-start.4
  74.5 26.1 %prefill.1 = bf16[8,64,1024]{2,1,0:T(8,128)(2,1)} custom-call(bf16[8,592,128]{2,1,0:T(8,128)(2,1)} %copy-done, bf16[4480,256]{1,0:T(8,128)(2,1)} %get-tuple-element.5.k_s, bf16[4480,256]{1,0:T(8,128)(2,1)} %get-tuple-element.6.v_s), custom_call_target="tpu_custom_call" | custom-call | flops 25999998976 | bytes 6000000 | tf_op jit(solution)/shard_map/prefill/pallas_call | solution.py:328
  100.5 4.6 %all-to-all-start.2 = ((bf16[8,64,1024]{2,1,0:T(8,128)(2,1)}), bf16[8,64,1024]{2,1,0:T(8,128)(2,1)S(1)}, u32[]{:S(2)}, u32[]{:S(2)}) async-start(bf16[8,64,1024]{2,1,0:T(8,128)(2,1)} %prefill.1), calls=%async_computation.2 | async-start | bytes 2097152 | tf_op jit(solution)/shard_map/all_to_all | solution.py:451
  105.2 0.5 finish.1
  105.7 0.6 reshape.45
  106.3 15.1 %all-to-all-done.2.in_ref = bf16[8,64,1024]{2,1,0:T(8,128)(2,1)S(1)} async-done(((bf16[8,64,1024]{2,1,0:T(8,128)(2,1)}), bf16[8,64,1024]{2,1,0:T(8,128)(2,1)S(1)}, u32[]{:S(2)}, u32[]{:S(2)}) %all-to-all-start.2) | async-done | bytes 1048608 | tf_op jit(solution)/shard_map/all_to_all | solution.py:451
  121.5 1.0 place.1
  (21 shorter events, 0.2 us)
Async XLA Ops:
  3.4 8.3 %copy-start.3 = (bf16[4,2,8192]{2,1,0:T(2,128)(2,1)S(1)}, bf16[4,2,8192]{2,1,0:T(2,128)(2,1)}, u32[]{:S(2)}) copy-start(bf16[4,2,8192]{2,1,0:T(2,128)(2,1)} %param.12) | copy-start | bytes 393220
  3.4 9.1 %copy-start.5 = (s32[4]{0:T(128)S(1)}, s32[4]{0:T(128)}, u32[]{:S(2)}) copy-start(s32[4]{0:T(128)} %param.15) | copy-start | bytes 52
  3.4 42.5 %all-to-all-start.1 = ((bf16[8,576,256]{2,1,0:T(8,128)(2,1)}), bf16[8,576,256]{2,1,0:T(8,128)(2,1)S(1)}, u32[]{:S(2)}, u32[]{:S(2)}) async-start(bf16[8,576,256]{2,1,0:T(8,128)(2,1)} %pack.1), calls=%async_computation.1 | async-start | bytes 4718592 | tf_op jit(solution)/shard_map/all_to_all | solution.py:439
  22.3 1.8 %collective-permute-start = (bf16[64,128]{1,0:T(8,128)(2,1)S(1)}, bf16[64,128]{1,0:T(8,128)(2,1)S(1)}, u32[]{:S(2)}, u32[]{:S(2)}) collective-permute-start(bf16[64,128]{1,0:T(8,128)(2,1)S(1)} %get-tuple-element.8), channel_id=1, source_target_pairs={{0,1},{1,0},{2,3},{3,2},{4,5},{5,4},{6,7},{7,6},{8,9},{9,8},{10,11... | collective-permute-start | bytes 49160 | tf_op jit(solution)/shard_map/ppermute | solution.py:428
  24.1 3.1 %collective-permute-start.1 = (bf16[128,128]{1,0:T(8,128)(2,1)S(1)}, bf16[128,128]{1,0:T(8,128)(2,1)S(1)}, u32[]{:S(2)}, u32[]{:S(2)}) collective-permute-start(bf16[128,128]{1,0:T(8,128)(2,1)S(1)} %pad_maximum_fusion.2), channel_id=1, source_target_pairs={{0,4},{1,5},{2,6},{3,7},{4,0},{5,1},{6,2},{7,3},{8,12},{9,13},{10,... | collective-permute-start | bytes 98312 | tf_op jit(solution)/shard_map/ppermute | solution.py:428
  27.2 5.0 %collective-permute-start.2 = (bf16[256,128]{1,0:T(8,128)(2,1)S(1)}, bf16[256,128]{1,0:T(8,128)(2,1)S(1)}, u32[]{:S(2)}, u32[]{:S(2)}) collective-permute-start(bf16[256,128]{1,0:T(8,128)(2,1)S(1)} %pad_maximum_fusion.1), channel_id=1, source_target_pairs={{0,8},{1,9},{2,10},{3,11},{4,12},{5,13},{6,14},{7,15},{8,0},{9,1},... | collective-permute-start | bytes 196616 | tf_op jit(solution)/shard_map/ppermute | solution.py:428
  45.9 1.4 %copy-start.2 = (bf16[8,576,256]{2,1,0:T(8,128)(2,1)}, bf16[8,576,256]{2,1,0:T(8,128)(2,1)S(1)}, u32[]{:S(2)}) copy-start(bf16[8,576,256]{2,1,0:T(8,128)(2,1)S(1)} %all-to-all-done.1.got_ref) | copy-start | bytes 7077892
  46.0 5.0 %collective-permute-start.3 = (bf16[512,128]{1,0:T(8,128)(2,1)S(1)}, bf16[512,128]{1,0:T(8,128)(2,1)S(1)}, u32[]{:S(2)}, u32[]{:S(2)}) collective-permute-start(bf16[512,128]{1,0:T(8,128)(2,1)S(1)} %maximum_add_fusion), channel_id=1, source_target_pairs={{0,2},{1,3},{2,0},{3,1},{4,6},{5,7},{6,4},{7,5},{8,10},{9,11},{10,... | collective-permute-start | bytes 393224 | tf_op jit(solution)/shard_map/ppermute | solution.py:428
  47.4 20.6 %all-to-all-start = ((bf16[8,592,128]{2,1,0:T(8,128)(2,1)}), bf16[8,592,128]{2,1,0:T(8,128)(2,1)S(1)}, u32[]{:S(2)}, u32[]{:S(2)}) async-start(bf16[8,592,128]{2,1,0:T(8,128)(2,1)} %query_res.1), calls=%async_computation | async-start | bytes 2424832 | tf_op jit(solution)/shard_map/all_to_all | solution.py:445
  68.0 6.5 %copy-start = (bf16[8,592,128]{2,1,0:T(8,128)(2,1)}, bf16[8,592,128]{2,1,0:T(8,128)(2,1)S(1)}, u32[]{:S(2)}) copy-start(bf16[8,592,128]{2,1,0:T(8,128)(2,1)S(1)} %all-to-all-done.got_q_ref.in_ref) | copy-start | bytes 3637252
  68.0 32.6 %all-to-all-start.3 = ((bf16[16,80,128]{2,1,0:T(8,128)(2,1)}), bf16[16,80,128]{2,1,0:T(8,128)(2,1)S(1)}, u32[]{:S(2)}, u32[]{:S(2)}) async-start(bf16[16,80,128]{2,1,0:T(8,128)(2,1)} %get-tuple-element.7), calls=%async_computation.3 | async-start | bytes 655360 | tf_op jit(solution)/shard_map/all_to_all | solution.py:449
  74.4 30.6 %copy-start.4 = (bf16[4,2,2048]{2,1,0:T(2,128)(2,1)S(1)}, bf16[4,2,2048]{2,1,0:T(2,128)(2,1)}, u32[]{:S(2)}) copy-start(bf16[4,2,2048]{2,1,0:T(2,128)(2,1)} %param.13) | copy-start | bytes 98308
  100.5 4.6 %copy-start.1 = (bf16[8,592,128]{2,1,0:T(8,128)(2,1)S(1)}, bf16[8,592,128]{2,1,0:T(8,128)(2,1)}, u32[]{:S(2)}) copy-start(bf16[8,592,128]{2,1,0:T(8,128)(2,1)} %copy-done) | copy-start | bytes 3637252
  100.5 20.9 %all-to-all-start.2 = ((bf16[8,64,1024]{2,1,0:T(8,128)(2,1)}), bf16[8,64,1024]{2,1,0:T(8,128)(2,1)S(1)}, u32[]{:S(2)}, u32[]{:S(2)}) async-start(bf16[8,64,1024]{2,1,0:T(8,128)(2,1)} %prefill.1), calls=%async_computation.2 | async-start | bytes 2097152 | tf_op jit(solution)/shard_map/all_to_all | solution.py:451

commit v4 on v3

--- a/solution.py
+++ b/solution.py
@@ -419,12 +419,10 @@
     )(parts)
 
 
-def spread_over(values, axis, size, before, got):
+def spread_over(values, axis, size, before):
     values = values + before[0, :1, :] * 0
     me = lax.axis_index(axis)
     for bit in BITS:
-        if bit == BITS[-1]:
-            values = values + got[0, :1, :HD] * 0
         other = lax.ppermute(values, axis, [(i, i ^ bit) for i in range(size)])
         upper = (me & bit) != 0
         values = jnp.concatenate(
@@ -443,7 +441,7 @@
     own_vecs = lax.dynamic_index_in_dim(dec_vecs, ctx, 0, keepdims=False)
     sent_q = query_res(lens - ctx * RES_DEV, tail_q[0], dec_vecs, res_kv)
     got_q = lax.all_to_all(sent_q, "ctx", split_axis=0, concat_axis=0, tiled=True)
-    all_vecs = spread_over(own_vecs, "grp", N_GRP, sent_q, got)
+    all_vecs = spread_over(own_vecs, "grp", N_GRP, sent_q)
 
     block_parts, keys, values = blocks(got, all_vecs)
     block_parts = lax.all_to_all(block_parts, "grp", split_axis=0, concat_axis=0, tiled=True)

time: 123 us -> 123 us (level)
  no operation moved by 1% of the time
where the time goes in v4:
time: 123 us
  Pallas kernels  49.2 us (40%)
  waiting for transfers between devices  37.7 us (31%)
  starting transfers between devices  29.1 us (24%)
  local copies, waits for them, and re-layouts  2.93 us (2%)
  other arithmetic  2.77 us (2%)
    pallas_call x1, Pallas kernels, prefill(): pl.pallas_call(prefill_kernel, grid=(N_CTX // STEP,), in_specs=[pl.BlockS...  26.1 us
    all_to_all x1, waiting for transfers between devices, local(): lax.all_to_all(parts, 'ctx', split_axis=0, concat_axis=0, tiled=True)  15.1 us
    all_to_all x1, waiting for transfers between devices, local(): got = lax.all_to_all(sent, 'ctx', split_axis=0, concat_axis=0, tiled=True)  12.8 us
    pallas_call x1, Pallas kernels, blocks(): pl.pallas_call(blocks_kernel, in_specs=[whole(pltpu.HBM), whole()], out_s...  11 us
    all_to_all x1, starting transfers between devices, local(): got = lax.all_to_all(sent, 'ctx', split_axis=0, concat_axis=0, tiled=True)  8.31 us
    pallas_call x1, Pallas kernels, query_res(): pl.pallas_call(query_res_kernel, grid=(KVH,), in_specs=[pl.BlockSpec(memo...  7.83 us
    all_to_all x1, starting transfers between devices, local(): lax.all_to_all(block_parts, 'grp', split_axis=0, concat_axis=0, tiled=True)  6.51 us
    ppermute x4, starting transfers between devices, spread_over(): other = lax.ppermute(values, axis, [(i, i ^ bit) for i in range(size)])  6.14 us
  transfers between devices with their start and end apart: 8, of which 6 were waited for; matrix products, arithmetic and copies ran while one was open for 3% of the time, Pallas kernels for 37%

profile of v4, /device:TPU:1, one launch (start us, length us, event | category | flops | bytes accessed | tf_op | source)
XLA Modules:
  0.0 122.6 jit_solution(2950006240567320194)
XLA Ops:
  0.6 2.7 %pack.1 = bf16[8,576,256]{2,1,0:T(8,128)(2,1)} custom-call(s32[35]{0:T(128)} %bitcast.28, s32[35]{0:T(128)} %bitcast.29, bf16[560,2048]{1,0:T(8,128)(2,1)} %bitcast.22), custom_call_target="tpu_custom_call" | custom-call | bytes 4600000 | tf_op jit(solution)/shard_map/pack/pallas_call | solution.py:130
  3.4 0.0 copy-start.3
  3.4 0.0 copy-start.5
  3.4 8.3 %all-to-all-start.1 = ((bf16[8,576,256]{2,1,0:T(8,128)(2,1)}), bf16[8,576,256]{2,1,0:T(8,128)(2,1)S(1)}, u32[]{:S(2)}, u32[]{:S(2)}) async-start(bf16[8,576,256]{2,1,0:T(8,128)(2,1)} %pack.1), calls=%async_computation.1 | async-start | bytes 4718592 | tf_op jit(solution)/shard_map/all_to_all | solution.py:437
  11.7 0.1 reshape.31
  11.8 0.7 copy.15
  12.5 0.5 broadcast_subtract_fusion.live_ref
  13.0 7.8 %query_res.1 = bf16[8,592,128]{2,1,0:T(8,128)(2,1)} custom-call(s32[4]{0:T(128)} %broadcast_subtract_fusion.live_ref, bf16[64,8192]{1,0:T(8,128)(2,1)} %bitcast.24, bf16[8,64,128]{2,1,0:T(8,128)(2,1)} %bitcast.25, bf16[4,128,2048]{2,1,0:T(8,128)(2,1)} %v_ref.1, bf16[4,128,2048]{2,1,0:T(8,128)(2,1)} %v_ref.1), custom_call_target="tpu_custom_call" | custom-call | flops 500000000 | bytes 4600000 | tf_op jit(solution)/shard_map/query_res/pallas_call | solution.py:176
  20.9 0.7 fusion.2
  21.5 0.7 broadcast_add_fusion
  22.2 1.0 collective-permute-start
  23.2 0.8 collective-permute-done
  24.1 1.4 %collective-permute-start.1 = (bf16[128,128]{1,0:T(8,128)(2,1)S(1)}, bf16[128,128]{1,0:T(8,128)(2,1)S(1)}, u32[]{:S(2)}, u32[]{:S(2)}) collective-permute-start(bf16[128,128]{1,0:T(8,128)(2,1)S(1)} %pad_maximum_fusion.3), channel_id=1, source_target_pairs={{0,4},{1,5},{2,6},{3,7},{4,0},{5,1},{6,2},{7,3},{8,12},{9,13},{10,... | collective-permute-start | bytes 98312 | tf_op jit(solution)/shard_map/ppermute | solution.py:426
  25.4 1.8 %collective-permute-done.1 = bf16[128,128]{1,0:T(8,128)(2,1)S(1)} collective-permute-done((bf16[128,128]{1,0:T(8,128)(2,1)S(1)}, bf16[128,128]{1,0:T(8,128)(2,1)S(1)}, u32[]{:S(2)}, u32[]{:S(2)}) %collective-permute-start.1) | collective-permute-done | bytes 32800 | tf_op jit(solution)/shard_map/ppermute | solution.py:426
  27.2 3.0 %collective-permute-start.2 = (bf16[256,128]{1,0:T(8,128)(2,1)S(1)}, bf16[256,128]{1,0:T(8,128)(2,1)S(1)}, u32[]{:S(2)}, u32[]{:S(2)}) collective-permute-start(bf16[256,128]{1,0:T(8,128)(2,1)S(1)} %pad_maximum_fusion.2), channel_id=1, source_target_pairs={{0,8},{1,9},{2,10},{3,11},{4,12},{5,13},{6,14},{7,15},{8,0},{9,1},... | collective-permute-start | bytes 196616 | tf_op jit(solution)/shard_map/ppermute | solution.py:426
  30.2 2.0 %collective-permute-done.2 = bf16[256,128]{1,0:T(8,128)(2,1)S(1)} collective-permute-done((bf16[256,128]{1,0:T(8,128)(2,1)S(1)}, bf16[256,128]{1,0:T(8,128)(2,1)S(1)}, u32[]{:S(2)}, u32[]{:S(2)}) %collective-permute-start.2) | collective-permute-done | bytes 65568 | tf_op jit(solution)/shard_map/ppermute | solution.py:426
  32.3 0.8 collective-permute-start.3
  33.1 12.8 %all-to-all-done.1.got_ref = bf16[8,576,256]{2,1,0:T(8,128)(2,1)S(1)} async-done(((bf16[8,576,256]{2,1,0:T(8,128)(2,1)}), bf16[8,576,256]{2,1,0:T(8,128)(2,1)S(1)}, u32[]{:S(2)}, u32[]{:S(2)}) %all-to-all-start.1) | async-done | bytes 2359328 | tf_op jit(solution)/shard_map/all_to_all | solution.py:437
  45.9 1.4 %copy-done.2 = bf16[8,576,256]{2,1,0:T(8,128)(2,1)} copy-done((bf16[8,576,256]{2,1,0:T(8,128)(2,1)}, bf16[8,576,256]{2,1,0:T(8,128)(2,1)S(1)}, u32[]{:S(2)}) %copy-start.2) | copy-done | bytes 2359320
  47.4 3.6 %all-to-all-start = ((bf16[8,592,128]{2,1,0:T(8,128)(2,1)}), bf16[8,592,128]{2,1,0:T(8,128)(2,1)S(1)}, u32[]{:S(2)}, u32[]{:S(2)}) async-start(bf16[8,592,128]{2,1,0:T(8,128)(2,1)} %query_res.1), calls=%async_computation | async-start | bytes 2424832 | tf_op jit(solution)/shard_map/all_to_all | solution.py:443
  51.0 0.1 broadcast_select_fusion.1
  51.0 0.7 pad_maximum_fusion.dq_ref
  51.7 11.0 %blocks.1 = (bf16[16,80,128]{2,1,0:T(8,128)(2,1)}, bf16[4480,256]{1,0:T(8,128)(2,1)}, bf16[4480,256]{1,0:T(8,128)(2,1)}) custom-call(bf16[8,576,256]{2,1,0:T(8,128)(2,1)} %copy-done.2, bf16[1024,128]{1,0:T(8,128)(2,1)} %pad_maximum_fusion.dq_ref), custom_call_target="tpu_custom_call" | custom-call | flops 8000000000 | bytes 3000000 | tf_op jit(solution)/shard_map/blocks/pallas_call | solution.py:282
  62.8 5.1 %all-to-all-done.got_q_ref.in_ref = bf16[8,592,128]{2,1,0:T(8,128)(2,1)S(1)} async-done(((bf16[8,592,128]{2,1,0:T(8,128)(2,1)}), bf16[8,592,128]{2,1,0:T(8,128)(2,1)S(1)}, u32[]{:S(2)}, u32[]{:S(2)}) %all-to-all-start) | async-done | bytes 1212448 | tf_op jit(solution)/shard_map/all_to_all | solution.py:443
  67.9 6.5 %all-to-all-start.3 = ((bf16[16,80,128]{2,1,0:T(8,128)(2,1)}), bf16[16,80,128]{2,1,0:T(8,128)(2,1)S(1)}, u32[]{:S(2)}, u32[]{:S(2)}) async-start(bf16[16,80,128]{2,1,0:T(8,128)(2,1)} %get-tuple-element.7), calls=%async_computation.3 | async-start | bytes 655360 | tf_op jit(solution)/shard_map/all_to_all | solution.py:447
  74.4 0.0 copy-start.4
  74.4 26.1 %prefill.1 = bf16[8,64,1024]{2,1,0:T(8,128)(2,1)} custom-call(bf16[8,592,128]{2,1,0:T(8,128)(2,1)} %copy-done, bf16[4480,256]{1,0:T(8,128)(2,1)} %get-tuple-element.5.k_s, bf16[4480,256]{1,0:T(8,128)(2,1)} %get-tuple-element.6.v_s), custom_call_target="tpu_custom_call" | custom-call | flops 25999998976 | bytes 6000000 | tf_op jit(solution)/shard_map/prefill/pallas_call | solution.py:328
  100.5 4.6 %all-to-all-start.2 = ((bf16[8,64,1024]{2,1,0:T(8,128)(2,1)}), bf16[8,64,1024]{2,1,0:T(8,128)(2,1)S(1)}, u32[]{:S(2)}, u32[]{:S(2)}) async-start(bf16[8,64,1024]{2,1,0:T(8,128)(2,1)} %prefill.1), calls=%async_computation.2 | async-start | bytes 2097152 | tf_op jit(solution)/shard_map/all_to_all | solution.py:449
  105.2 0.5 finish.1
  105.7 0.6 reshape.36
  106.3 15.1 %all-to-all-done.2.in_ref = bf16[8,64,1024]{2,1,0:T(8,128)(2,1)S(1)} async-done(((bf16[8,64,1024]{2,1,0:T(8,128)(2,1)}), bf16[8,64,1024]{2,1,0:T(8,128)(2,1)S(1)}, u32[]{:S(2)}, u32[]{:S(2)}) %all-to-all-start.2) | async-done | bytes 1048608 | tf_op jit(solution)/shard_map/all_to_all | solution.py:449
  121.5 1.0 place.1
  (20 shorter events, 0.1 us)
Async XLA Ops:
  3.4 8.3 %copy-start.3 = (bf16[4,2,8192]{2,1,0:T(2,128)(2,1)S(1)}, bf16[4,2,8192]{2,1,0:T(2,128)(2,1)}, u32[]{:S(2)}) copy-start(bf16[4,2,8192]{2,1,0:T(2,128)(2,1)} %param.12) | copy-start | bytes 393220
  3.4 9.1 %copy-start.5 = (s32[4]{0:T(128)S(1)}, s32[4]{0:T(128)}, u32[]{:S(2)}) copy-start(s32[4]{0:T(128)} %param.15) | copy-start | bytes 52
  3.4 42.5 %all-to-all-start.1 = ((bf16[8,576,256]{2,1,0:T(8,128)(2,1)}), bf16[8,576,256]{2,1,0:T(8,128)(2,1)S(1)}, u32[]{:S(2)}, u32[]{:S(2)}) async-start(bf16[8,576,256]{2,1,0:T(8,128)(2,1)} %pack.1), calls=%async_computation.1 | async-start | bytes 4718592 | tf_op jit(solution)/shard_map/all_to_all | solution.py:437
  22.2 1.8 %collective-permute-start = (bf16[64,128]{1,0:T(8,128)(2,1)S(1)}, bf16[64,128]{1,0:T(8,128)(2,1)S(1)}, u32[]{:S(2)}, u32[]{:S(2)}) collective-permute-start(bf16[64,128]{1,0:T(8,128)(2,1)S(1)} %get-tuple-element.8), channel_id=1, source_target_pairs={{0,1},{1,0},{2,3},{3,2},{4,5},{5,4},{6,7},{7,6},{8,9},{9,8},{10,11... | collective-permute-start | bytes 49160 | tf_op jit(solution)/shard_map/ppermute | solution.py:426
  24.1 3.1 %collective-permute-start.1 = (bf16[128,128]{1,0:T(8,128)(2,1)S(1)}, bf16[128,128]{1,0:T(8,128)(2,1)S(1)}, u32[]{:S(2)}, u32[]{:S(2)}) collective-permute-start(bf16[128,128]{1,0:T(8,128)(2,1)S(1)} %pad_maximum_fusion.3), channel_id=1, source_target_pairs={{0,4},{1,5},{2,6},{3,7},{4,0},{5,1},{6,2},{7,3},{8,12},{9,13},{10,... | collective-permute-start | bytes 98312 | tf_op jit(solution)/shard_map/ppermute | solution.py:426
  27.2 5.0 %collective-permute-start.2 = (bf16[256,128]{1,0:T(8,128)(2,1)S(1)}, bf16[256,128]{1,0:T(8,128)(2,1)S(1)}, u32[]{:S(2)}, u32[]{:S(2)}) collective-permute-start(bf16[256,128]{1,0:T(8,128)(2,1)S(1)} %pad_maximum_fusion.2), channel_id=1, source_target_pairs={{0,8},{1,9},{2,10},{3,11},{4,12},{5,13},{6,14},{7,15},{8,0},{9,1},... | collective-permute-start | bytes 196616 | tf_op jit(solution)/shard_map/ppermute | solution.py:426
  32.3 18.7 %collective-permute-start.3 = (bf16[512,128]{1,0:T(8,128)(2,1)S(1)}, bf16[512,128]{1,0:T(8,128)(2,1)S(1)}, u32[]{:S(2)}, u32[]{:S(2)}) collective-permute-start(bf16[512,128]{1,0:T(8,128)(2,1)S(1)} %pad_maximum_fusion.1), channel_id=1, source_target_pairs={{0,2},{1,3},{2,0},{3,1},{4,6},{5,7},{6,4},{7,5},{8,10},{9,11},{10,... | collective-permute-start | bytes 393224 | tf_op jit(solution)/shard_map/ppermute | solution.py:426
  45.9 1.4 %copy-start.2 = (bf16[8,576,256]{2,1,0:T(8,128)(2,1)}, bf16[8,576,256]{2,1,0:T(8,128)(2,1)S(1)}, u32[]{:S(2)}) copy-start(bf16[8,576,256]{2,1,0:T(8,128)(2,1)S(1)} %all-to-all-done.1.got_ref) | copy-start | bytes 7077892
  47.4 20.5 %all-to-all-start = ((bf16[8,592,128]{2,1,0:T(8,128)(2,1)}), bf16[8,592,128]{2,1,0:T(8,128)(2,1)S(1)}, u32[]{:S(2)}, u32[]{:S(2)}) async-start(bf16[8,592,128]{2,1,0:T(8,128)(2,1)} %query_res.1), calls=%async_computation | async-start | bytes 2424832 | tf_op jit(solution)/shard_map/all_to_all | solution.py:443
  67.9 6.5 %copy-start = (bf16[8,592,128]{2,1,0:T(8,128)(2,1)}, bf16[8,592,128]{2,1,0:T(8,128)(2,1)S(1)}, u32[]{:S(2)}) copy-start(bf16[8,592,128]{2,1,0:T(8,128)(2,1)S(1)} %all-to-all-done.got_q_ref.in_ref) | copy-start | bytes 3637252
  67.9 32.6 %all-to-all-start.3 = ((bf16[16,80,128]{2,1,0:T(8,128)(2,1)}), bf16[16,80,128]{2,1,0:T(8,128)(2,1)S(1)}, u32[]{:S(2)}, u32[]{:S(2)}) async-start(bf16[16,80,128]{2,1,0:T(8,128)(2,1)} %get-tuple-element.7), calls=%async_computation.3 | async-start | bytes 655360 | tf_op jit(solution)/shard_map/all_to_all | solution.py:447
  74.4 30.7 %copy-start.4 = (bf16[4,2,2048]{2,1,0:T(2,128)(2,1)S(1)}, bf16[4,2,2048]{2,1,0:T(2,128)(2,1)}, u32[]{:S(2)}) copy-start(bf16[4,2,2048]{2,1,0:T(2,128)(2,1)} %param.13) | copy-start | bytes 98308
  100.5 4.7 %copy-start.1 = (bf16[8,592,128]{2,1,0:T(8,128)(2,1)S(1)}, bf16[8,592,128]{2,1,0:T(8,128)(2,1)}, u32[]{:S(2)}) copy-start(bf16[8,592,128]{2,1,0:T(8,128)(2,1)} %copy-done) | copy-start | bytes 3637252
  100.5 21.0 %all-to-all-start.2 = ((bf16[8,64,1024]{2,1,0:T(8,128)(2,1)}), bf16[8,64,1024]{2,1,0:T(8,128)(2,1)S(1)}, u32[]{:S(2)}, u32[]{:S(2)}) async-start(bf16[8,64,1024]{2,1,0:T(8,128)(2,1)} %prefill.1), calls=%async_computation.2 | async-start | bytes 2097152 | tf_op jit(solution)/shard_map/all_to_all | solution.py:449
